TPU v7x, 32 devices: a whole 2x2x4 slice. The times are simulated.
32 devices in a mesh: expo: 4 (over z), sky: 8 (over y, x, core).
Axes of the slice: x: 2, y: 2, z: 4, core: 2. Of those that a mesh axis runs over, the one named last changes fastest.
Arguments:
- samples: bfloat16 [512, 32, 256], P('sky'), may hold values from -0.75 to 0.75
- basis: bfloat16 [256, 1024], replicated, may hold values from -3 to 3
- operators: bfloat16 [256, 1024, 1024], P(('expo', 'sky')), may hold values from -0.1875 to 0.1875
- cutouts: float32 [256, 16, 1024], P(('expo', 'sky')), may hold values from -6 to 6
- pixel_weights: float32 [256, 16, 1024], P(('expo', 'sky')), may hold values from 0.25 to 4
- detections: int32 [4, 8, 8, 24], P('expo', 'sky'), may hold values from -1 to 63, as said below
- intersections: int32 [256, 16], P(('expo', 'sky')), may hold values from -1 to 191, as said below
Outputs:
- loglik: float32 [512, 32], P('sky', 'expo')
- coeff_grads: float32 [512, 32, 256], P('sky', 'expo')
Inputs may be any that keep to these rules, and one draw needn't show every extreme that they name: In detections[e, s, c], the live slots (values 0 or more) come first; -1 marks the rest. For every device (e, c), the live slots over all s total exactly 96, and one s fills all 24. A galaxy may stand in several slots. `intersections`: on device (e, c), a slot r = s * 24 + j is live exactly when detections[e, s, c, j] >= 0, and each live slot stands at exactly one position of the device's tiles; -1 marks empty positions. One tile of every device has all 16 positions filled.
All inputs are finite; a program needn't handle non-finite values.
Results may differ from a plain program's by a relative error of at most 0.0017.
Values may be sent and summed in bfloat16 or wider, within the bound.
A program may use at most 128 MiB of HBM per device.

v0:
```python
import jax
import jax.numpy as jnp
from jax import lax
from jax.sharding import PartitionSpec as P


def galaxy_sums(listed, values, galaxy_count):
    flat_list = listed.reshape(-1)
    onehot = (flat_list[None, :] == jnp.arange(galaxy_count, dtype=jnp.int32)[:, None]).astype(
        jnp.float32
    )
    return jnp.dot(onehot, values.reshape(flat_list.shape[0], -1), precision=lax.Precision.HIGHEST)


def per_device(samples, basis, operators, cutouts, pixel_weights, detections, intersections):
    tiles_here, tile_cap, pixels = cutouts.shape
    coeff_dim = basis.shape[0]
    galaxy_count, sample_count, _unused = samples.shape
    sky_count = lax.axis_size("sky")
    send_cap = detections.shape[3]
    slot_count = sky_count * send_cap
    sent_rows = detections.reshape(sky_count, send_cap)
    flat_samples = samples.reshape(galaxy_count, sample_count * coeff_dim)
    outgoing = jnp.take(flat_samples, jnp.maximum(sent_rows, 0), axis=0)
    incoming = lax.all_to_all(outgoing, "sky", split_axis=0, concat_axis=0, tiled=True)
    incoming = incoming.reshape(slot_count, sample_count * coeff_dim)
    live = intersections >= 0
    picked = jnp.take(incoming, jnp.maximum(intersections, 0), axis=0).reshape(-1, coeff_dim)
    rendered = jnp.dot(picked, basis, preferred_element_type=jnp.float32).astype(jnp.bfloat16)
    rendered = rendered.reshape(tiles_here, tile_cap * sample_count, pixels)
    model = jnp.einsum("tnp,tpq->tnq", rendered, operators, preferred_element_type=jnp.float32)
    model = model.reshape(tiles_here, tile_cap, sample_count, pixels)
    resid = model - cutouts[:, :, None, :]
    weighted = pixel_weights[:, :, None, :] * resid
    pair_like = -0.5 / pixels * jnp.sum(weighted * resid, axis=-1)
    scaled = weighted.astype(jnp.bfloat16).reshape(tiles_here, tile_cap * sample_count, pixels)
    backed = jnp.einsum(
        "tnq,tpq->tnp", scaled, operators, preferred_element_type=jnp.float32
    ).astype(jnp.bfloat16)
    pair_grad = (
        -1.0
        / pixels
        * lax.dot_general(
            backed.reshape(-1, pixels),
            basis,
            (((1,), (1,)), ((), ())),
            preferred_element_type=jnp.float32,
        )
    )
    target = jnp.where(live, intersections, slot_count).reshape(-1)
    slot_grads = jnp.zeros((slot_count, sample_count * coeff_dim), jnp.float32)
    slot_grads = slot_grads.at[target].set(
        pair_grad.reshape(tiles_here * tile_cap, sample_count * coeff_dim), mode="drop"
    )
    slot_like = jnp.zeros((slot_count, sample_count), jnp.float32)
    slot_like = slot_like.at[target].set(
        pair_like.reshape(tiles_here * tile_cap, sample_count), mode="drop"
    )
    back_grads, back_like = (
        lax.all_to_all(
            slot_grads.reshape(sky_count, send_cap, sample_count * coeff_dim),
            "sky",
            split_axis=0,
            concat_axis=0,
            tiled=True,
        ),
        lax.all_to_all(
            slot_like.reshape(sky_count, send_cap, sample_count),
            "sky",
            split_axis=0,
            concat_axis=0,
            tiled=True,
        ),
    )
    grad_part = galaxy_sums(sent_rows, back_grads, galaxy_count).reshape(
        galaxy_count, sample_count, coeff_dim
    )
    like_part = galaxy_sums(sent_rows, back_like, galaxy_count)
    like_out, grad_out = (
        lax.psum_scatter(like_part, "expo", scatter_dimension=1, tiled=True),
        lax.psum_scatter(grad_part, "expo", scatter_dimension=1, tiled=True),
    )
    return (like_out, grad_out)


def solution(mesh):
    placed = (
        P("sky", None, None),
        P(),
        P(("expo", "sky"), None, None),
        P(("expo", "sky"), None, None),
        P(("expo", "sky"), None, None),
        P("expo", "sky", None, None),
        P(("expo", "sky"), None),
    )
    return jax.shard_map(
        per_device,
        mesh=mesh,
        in_specs=placed,
        out_specs=(P("sky", "expo"), P("sky", "expo", None)),
        check_vma=False,
    )
```

profile of v0, /device:TPU:0, one launch (start us, length us, event | category | flops | bytes accessed | tf_op | source)
XLA Modules:
  0.0 269.7 jit_solution(18349890021706146727)
XLA Ops:
  7.2 0.7 broadcast_maximum_fusion
  8.6 1.9 copy.15
  10.6 4.2 %gather_fusion = bf16[192,8192]{1,0:T(8,128)(2,1)} fusion(bf16[64,8192]{1,0:T(8,128)(2,1)S(1)} %bitcast.52, s32[1024]{0:T(1024)S(1)} %pad_clamp_fusion.1), kind=kCustom, calls=%fused_computation | custom fusion | bytes 6292224 | tf_op jit(solution)/shard_map/jit(_take)/gather | solution.py:24
  14.8 3.9 %broadcast_select_fusion = bf16[8,24,8192]{2,1,0:T(8,128)(2,1)} fusion(bf16[8,24,8192]{2,1,0:T(8,128)(2,1)} %bitcast.55, pred[8,24]{1,0:T(8,128)(4,1)S(1)} %compare_bitcast_fusion), kind=kLoop, calls=%fused_computation.17 | loop fusion | flops 1572864 | bytes 6291648 | tf_op jit(solution)/shard_map/jit(_take)/select_n | solution.py:24
  18.7 5.2 %all-to-all-start = ((bf16[8,24,8192]{2,1,0:T(8,128)(2,1)}), bf16[8,24,8192]{2,1,0:T(8,128)(2,1)}, u32[]{:S(2)}, u32[]{:S(2)}) async-start(bf16[8,24,8192]{2,1,0:T(8,128)(2,1)} %broadcast_select_fusion), calls=%async_computation | async-start | bytes 6291456 | tf_op jit(solution)/shard_map/all_to_all | solution.py:25
  24.1 37.8 %all-to-all-done = bf16[8,24,8192]{2,1,0:T(8,128)(2,1)} async-done(((bf16[8,24,8192]{2,1,0:T(8,128)(2,1)}), bf16[8,24,8192]{2,1,0:T(8,128)(2,1)}, u32[]{:S(2)}, u32[]{:S(2)}) %all-to-all-start) | async-done | bytes 3145760 | tf_op jit(solution)/shard_map/all_to_all | solution.py:25
  61.9 6.1 %gather_fusion.1 = bf16[128,8192]{1,0:T(8,128)(2,1)S(1)} fusion(bf16[192,8192]{1,0:T(8,128)(2,1)} %bitcast.4, s32[1024]{0:T(1024)S(1)} %pad_clamp_fusion), kind=kCustom, calls=%fused_computation.1 | custom fusion | bytes 4194816 | tf_op jit(solution)/shard_map/jit(_take)/gather | solution.py:28
  68.0 1.6 broadcast_select_fusion.1
  69.6 2.9 %select_n.37 = bf16[4096,256]{1,0:T(8,128)(2,1)S(1)} reshape(bf16[8,16,8192]{2,1,0:T(8,128)(2,1)} %broadcast_select_fusion.1) | data formatting | bytes 4194304 | tf_op jit(solution)/shard_map/jit(_take)/select_n | solution.py:28
  72.5 5.6 %convolution_convert_fusion = bf16[4096,1024]{1,0:T(8,128)(2,1)} fusion(bf16[4096,256]{1,0:T(8,128)(2,1)S(1)} %select_n.37, bf16[256,1024]{1,0:T(8,128)(2,1)S(1)} %copy-done), kind=kOutput, calls=%fused_computation.9 | convolution fusion | flops 2151677952 | bytes 11010048 | tf_op jit(solution)/shard_map/dot_general | solution.py:29
  78.1 19.0 %fusion = (bf16[8,512,1024]{2,1,0:T(8,128)(2,1)}, f32[8,512]{1,0:T(8,128)S(1)}) fusion(f32[8,16,1024]{2,1,0:T(8,128)S(1)} %copy-done.1, f32[8,16,1024]{2,1,0:T(8,128)} %param.11, bf16[8,512,1024]{2,1,0:T(8,128)(2,1)} %bitcast.53, bf16[8,1024,1024]{2,1,0:T(8,128)(2,1)} %param.9), kind=kOutput, calls=%fused_computation.6 | convolution fusion | flops 8610902016 | bytes 34619392 | tf_op jit(solution)/shard_map/tnp,tpq->tnq/dot_general | solution.py:31
  97.1 15.7 %convolution_convert_fusion.1 = bf16[8,512,1024]{2,1,0:T(8,128)(2,1)} fusion(bf16[8,512,1024]{2,1,0:T(8,128)(2,1)} %get-tuple-element.8, bf16[8,1024,1024]{2,1,0:T(8,128)(2,1)} %param.9), kind=kOutput, calls=%fused_computation.10 | convolution fusion | flops 8594128896 | bytes 33554432 | tf_op jit(solution)/shard_map/tnq,tpq->tnp/dot_general | solution.py:37
  112.8 7.7 %convolution_multiply_fusion = f32[4096,256]{1,0:T(8,128)} fusion(bf16[4096,1024]{1,0:T(8,128)(2,1)} %bitcast.60, bf16[256,1024]{1,0:T(8,128)(2,1)S(1)} %copy-done), kind=kOutput, calls=%fused_computation.14 | convolution fusion | flops 2148532224 | bytes 13107200 | tf_op jit(solution)/shard_map/dot_general | solution.py:43
  120.5 5.0 %reshape.150 = f32[128,8192]{1,0:T(8,128)} reshape(f32[4096,256]{1,0:T(8,128)} %convolution_multiply_fusion) | data formatting | bytes 8388608 | tf_op jit(solution)/shard_map/reshape | solution.py:53
  125.4 7.5 %scatter_custom_fusion.1 = f32[192,8192]{1,0:T(8,128)} fusion(s32[128]{0:T(128)S(1)} %fusion.15, f32[128,8192]{1,0:T(8,128)} %reshape.150, f32[]{:T(128)} %constant.22.clone.1), kind=kCustom, calls=%fused_computation.15 | custom fusion | bytes 6291968 | tf_op jit(solution)/shard_map/scatter | solution.py:52
  133.0 4.9 %all-to-all-start.2 = ((f32[8,24,8192]{2,1,0:T(8,128)}), f32[8,24,8192]{2,1,0:T(8,128)}, u32[]{:S(2)}, u32[]{:S(2)}) async-start(f32[8,24,8192]{2,1,0:T(8,128)} %bitcast.54), calls=%async_computation.2 | async-start | bytes 12582912 | tf_op jit(solution)/shard_map/all_to_all | solution.py:60
  138.2 71.2 %all-to-all-done.2 = f32[8,24,8192]{2,1,0:T(8,128)} async-done(((f32[8,24,8192]{2,1,0:T(8,128)}), f32[8,24,8192]{2,1,0:T(8,128)}, u32[]{:S(2)}, u32[]{:S(2)}) %all-to-all-start.2) | async-done | bytes 6291488 | tf_op jit(solution)/shard_map/all_to_all | solution.py:60
  209.4 6.8 %fusion.3 = f32[64,32,256]{2,0,1:T(8,128)} fusion(f32[24,32,8,256]{3,2,1,0:T(8,128)} %bitcast.17, s32[192]{0:T(256)S(1)} %eq.8), kind=kOutput, calls=%fused_computation.11 | convolution fusion | flops 1207971840 | bytes 8389376 | tf_op jit(solution)/shard_map/dot_general | solution.py:12
  216.3 0.9 scatter_custom_fusion
  217.9 3.3 %all-to-all-start.1 = ((f32[8,1,768]{2,1,0:T(1,128)}), f32[8,1,768]{2,1,0:T(1,128)S(1)}, u32[]{:S(2)}, u32[]{:S(2)}) async-start(f32[8,1,768]{2,1,0:T(1,128)} %reshape.164), calls=%async_computation.1 | async-start | bytes 49152 | tf_op jit(solution)/shard_map/all_to_all | solution.py:67
  222.6 3.5 %all-to-all-done.1 = f32[8,1,768]{2,1,0:T(1,128)S(1)} async-done(((f32[8,1,768]{2,1,0:T(1,128)}), f32[8,1,768]{2,1,0:T(1,128)S(1)}, u32[]{:S(2)}, u32[]{:S(2)}) %all-to-all-start.1) | async-done | bytes 24608 | tf_op jit(solution)/shard_map/all_to_all | solution.py:67
  227.6 21.1 %all-reduce = f32[64,32]{0,1:T(8,128)S(1)} all-reduce(f32[64,32]{0,1:T(8,128)S(1)} %fusion.9), channel_id=2, replica_groups=mesh['expo'=4,'sky'=8] {'expo'}, use_global_device_ids=true, to_apply=%region_2.3.clone | all-reduce | flops 2048 | bytes 16384
  249.2 11.5 %reduce-scatter.2.cloned.1.call-done = f32[64,8,256]{2,0,1:T(8,128)} async-done(((f32[64,32,256]{2,0,1:T(8,128)}), f32[64,8,256]{2,0,1:T(8,128)}) %reduce-scatter.2.cloned.1.call-update) | async-done | bytes 524304 | tf_op jit(solution)/shard_map/reduce_scatter | solution.py:81
  260.7 2.1 copy.13
  (31 shorter events, 4.9 us)
Async XLA Ops:
  7.2 65.3 %copy-start = (bf16[256,1024]{1,0:T(8,128)(2,1)S(1)}, bf16[256,1024]{1,0:T(8,128)(2,1)}, u32[]{:S(2)}) copy-start(bf16[256,1024]{1,0:T(8,128)(2,1)} %param.8) | copy-start | bytes 1572868
  14.8 9.1 %copy-start.3 = (s32[8,16]{1,0:T(8,128)S(1)}, s32[8,16]{1,0:T(8,128)}, u32[]{:S(2)}) copy-start(s32[8,16]{1,0:T(8,128)} %param.13) | copy-start | bytes 1540
  18.7 43.2 %all-to-all-start = ((bf16[8,24,8192]{2,1,0:T(8,128)(2,1)}), bf16[8,24,8192]{2,1,0:T(8,128)(2,1)}, u32[]{:S(2)}, u32[]{:S(2)}) async-start(bf16[8,24,8192]{2,1,0:T(8,128)(2,1)} %broadcast_select_fusion), calls=%async_computation | async-start | bytes 6291456 | tf_op jit(solution)/shard_map/all_to_all | solution.py:25
  72.5 5.6 %copy-start.1 = (f32[8,16,1024]{2,1,0:T(8,128)S(1)}, f32[8,16,1024]{2,1,0:T(8,128)}, u32[]{:S(2)}) copy-start(f32[8,16,1024]{2,1,0:T(8,128)} %param.10) | copy-start | bytes 1572868
  133.0 5.2 %copy-start.2 = (s32[1,1,8,24]{3,2,1,0:T(8,128)S(1)}, s32[1,1,8,24]{3,2,1,0:T(8,128)}, u32[]{:S(2)}) copy-start(s32[1,1,8,24]{3,2,1,0:T(8,128)} %param.12) | copy-start | bytes 2308
  133.0 76.5 %all-to-all-start.2 = ((f32[8,24,8192]{2,1,0:T(8,128)}), f32[8,24,8192]{2,1,0:T(8,128)}, u32[]{:S(2)}, u32[]{:S(2)}) async-start(f32[8,24,8192]{2,1,0:T(8,128)} %bitcast.54), calls=%async_computation.2 | async-start | bytes 12582912 | tf_op jit(solution)/shard_map/all_to_all | solution.py:60
  137.8 83.5 %copy-start.4 = (u32[32]{0:T(128)S(1)}, u32[32]{0:T(128)}, u32[]{:S(2)}) copy-start(u32[32]{0:T(128)} %constant.53) | copy-start | bytes 388
  137.8 122.9 %reduce-scatter.2.cloned.1.call-start = ((), (), s32[]{:S(2)}) async-start(), calls=%async_computation.4 | async-start | bytes 2621440 | tf_op jit(solution)/shard_map/reduce_scatter | solution.py:81
  217.9 8.1 %all-to-all-start.1 = ((f32[8,1,768]{2,1,0:T(1,128)}), f32[8,1,768]{2,1,0:T(1,128)S(1)}, u32[]{:S(2)}, u32[]{:S(2)}) async-start(f32[8,1,768]{2,1,0:T(1,128)} %reshape.164), calls=%async_computation.1 | async-start | bytes 49152 | tf_op jit(solution)/shard_map/all_to_all | solution.py:67
Sparse Core Ops, SparseCore 0:
  216.4 44.3 reduce-scatter.1
where the time goes:
time: 271 us; the launch traced here: 270 us
  waiting for transfers between devices  124 us (46%)
  matrix products  55 us (20%)
  local copies, waits for them, and re-layouts  33.4 us (12%)
  blocking collectives  21.1 us (8%)
  between operations  14.8 us (5%)
  starting transfers between devices  13.7 us (5%)
  other arithmetic  7.72 us (3%)
    all_to_all x1, waiting for transfers between devices, per_device(): lax.all_to_all(slot_grads.reshape(sky_count, send_cap, sample_count * coe...  71.2 us
    all_to_all x1, waiting for transfers between devices, per_device(): lax.all_to_all(outgoing, 'sky', split_axis=0, concat_axis=0, tiled=True)  37.8 us
    unnamed x1, blocking collectives  21.1 us
    dot_general x1, matrix products, per_device(): jnp.einsum('tnp,tpq->tnq', rendered, operators, preferred_element_type=jn...  19 us
    dot_general x1, matrix products, per_device(): jnp.einsum('tnq,tpq->tnp', scaled, operators, preferred_element_type=jnp....  15.7 us
    reduce_scatter x1, waiting for transfers between devices, per_device(): lax.psum_scatter(grad_part, 'expo', scatter_dimension=1, tiled=True)  11.5 us
    dot_general x1, matrix products, per_device(): lax.dot_general(backed.reshape(-1, pixels), basis, (((1,), (1,)), ((), ()...  7.7 us
    scatter x1, local copies, waits for them, and re-layouts, per_device(): slot_grads.at[target]  7.5 us
  transfers between devices with their start and end apart: 4, of which 4 were waited for; matrix products, arithmetic and copies ran while one was open for 2% of the time, Pallas kernels for 0%

commit v1 on v0

v1 whole, which is shorter than its diff:
```python
import functools

import jax
import jax.numpy as jnp
from jax import lax
from jax.experimental import pallas as pl
from jax.experimental.pallas import tpu as pltpu
from jax.sharding import PartitionSpec as P

CHUNKS = 2
VMEM_BYTES = 48 * 1024 * 1024


def whole_vmem():
    return pl.BlockSpec(memory_space=pltpu.VMEM)


def gather_kernel(chunk, expo_count, listed_ref, samples_ref, out_ref, held):
    galaxy_count, rows, coeff_dim = held.shape
    sample_count = samples_ref.shape[0] // galaxy_count
    share = sample_count // expo_count
    part = share // CHUNKS
    group = 8
    out_row = lax.broadcasted_iota(jnp.int32, (group * rows, group * sample_count), 0)
    in_row = lax.broadcasted_iota(jnp.int32, (group * rows, group * sample_count), 1)
    within = out_row % rows
    wanted = (
        (out_row // rows) * sample_count
        + (within // part) * share
        + chunk * part
        + within % part
    )
    select = jnp.where(in_row == wanted, 1.0, 0.0).astype(jnp.bfloat16)
    for b in range(galaxy_count // group):
        block = samples_ref[b * group * sample_count : (b + 1) * group * sample_count, :]
        picked = jnp.dot(select, block, preferred_element_type=jnp.float32).astype(jnp.bfloat16)
        held[b * group : (b + 1) * group] = picked.reshape(group, rows, coeff_dim)

    @pl.loop(0, out_ref.shape[0], unroll=8)
    def _(slot):
        out_ref[slot] = held[jnp.maximum(listed_ref[slot], 0)]


def gather_slots(chunk, expo_count, listed, flat_samples, galaxy_count):
    rows = flat_samples.shape[0] // galaxy_count // CHUNKS
    coeff_dim = flat_samples.shape[1]
    return pl.pallas_call(
        functools.partial(gather_kernel, chunk, expo_count),
        out_shape=jax.ShapeDtypeStruct((listed.shape[0], rows, coeff_dim), jnp.bfloat16),
        in_specs=[pl.BlockSpec(memory_space=pltpu.SMEM), whole_vmem()],
        out_specs=whole_vmem(),
        scratch_shapes=[pltpu.VMEM((galaxy_count, rows, coeff_dim), jnp.bfloat16)],
        compiler_params=pltpu.CompilerParams(vmem_limit_bytes=VMEM_BYTES),
        cost_estimate=pl.CostEstimate(flops=10**8, bytes_accessed=3 * 10**6, transcendentals=0),
        name="gather_slots",
    )(listed, flat_samples)


def pair_kernel(inter_ref, incoming_ref, basis_ref, op_ref, cut_ref, weight_ref, grad_ref, like_ref, picked):
    tile = pl.program_id(0)
    cap, pixels = cut_ref.shape[1:]
    rows = incoming_ref.shape[1]

    @pl.when(tile == 0)
    def _():
        grad_ref[...] = jnp.zeros_like(grad_ref)

    for q in range(cap):
        picked[q * rows : (q + 1) * rows] = incoming_ref[jnp.maximum(inter_ref[tile, q], 0)]
    rendered = jnp.dot(picked[...], basis_ref[...], preferred_element_type=jnp.float32)
    rendered = rendered.astype(jnp.bfloat16)
    model = jnp.dot(rendered, op_ref[0], preferred_element_type=jnp.float32)
    resid = model.reshape(cap, rows, pixels) - cut_ref[0][:, None, :]
    weighted = weight_ref[0][:, None, :] * resid
    like_ref[0] = -0.5 / pixels * jnp.sum(weighted * resid, axis=-1)
    scaled = weighted.astype(jnp.bfloat16).reshape(cap * rows, pixels)
    last = (((1,), (1,)), ((), ()))
    backed = lax.dot_general(scaled, op_ref[0], last, preferred_element_type=jnp.float32)
    backed = backed.astype(jnp.bfloat16)
    grad = lax.dot_general(backed, basis_ref[...], last, preferred_element_type=jnp.float32)
    grad = (-1.0 / pixels * grad).astype(jnp.bfloat16)
    for q in range(cap):
        slot = inter_ref[tile, q]

        @pl.when(slot >= 0)
        def _():
            grad_ref[slot] = grad[q * rows : (q + 1) * rows]


def pair_terms(intersections, incoming, basis, operators, cutouts, pixel_weights):
    tiles, cap, pixels = cutouts.shape
    slots, rows, coeff_dim = incoming.shape
    flops = 4 * tiles * cap * rows * pixels * (pixels + coeff_dim)
    fixed = lambda t, inter: (0, 0, 0)
    moving = lambda t, inter: (t, 0, 0)
    return pl.pallas_call(
        pair_kernel,
        grid_spec=pltpu.PrefetchScalarGridSpec(
            num_scalar_prefetch=1,
            grid=(tiles,),
            in_specs=[
                pl.BlockSpec((slots, rows, coeff_dim), fixed),
                pl.BlockSpec((coeff_dim, pixels), lambda t, inter: (0, 0)),
                pl.BlockSpec((1, pixels, pixels), moving),
                pl.BlockSpec((1, cap, pixels), moving),
                pl.BlockSpec((1, cap, pixels), moving),
            ],
            out_specs=[
                pl.BlockSpec((slots, rows, coeff_dim), fixed),
                pl.BlockSpec((1, cap, rows), moving),
            ],
            scratch_shapes=[pltpu.VMEM((cap * rows, coeff_dim), jnp.bfloat16)],
        ),
        out_shape=[
            jax.ShapeDtypeStruct((slots, rows, coeff_dim), jnp.bfloat16),
            jax.ShapeDtypeStruct((tiles, cap, rows), jnp.float32),
        ],
        compiler_params=pltpu.CompilerParams(vmem_limit_bytes=VMEM_BYTES),
        cost_estimate=pl.CostEstimate(
            flops=flops, bytes_accessed=2 * operators.size + 4 * incoming.size, transcendentals=0
        ),
        name="pair_terms",
    )(intersections, incoming, basis, operators, cutouts, pixel_weights)


def sum_kernel(listed_ref, back_ref, out_ref, total):
    galaxy_count = total.shape[0] - 8
    expo_count = out_ref.shape[0]
    rows, coeff_dim = total.shape[1:]
    part = rows // expo_count
    total[...] = jnp.zeros_like(total)

    @pl.loop(0, back_ref.shape[0], unroll=8)
    def _(slot):
        listed = listed_ref[slot]
        place = jnp.where(listed >= 0, listed, galaxy_count)
        total[place] += back_ref[slot].astype(jnp.float32)

    for e in range(expo_count):
        mine = total[:galaxy_count, e * part : (e + 1) * part, :]
        out_ref[e] = mine.reshape(galaxy_count * part, coeff_dim)


def sum_galaxies(listed, back, galaxy_count, expo_count):
    slots, rows, coeff_dim = back.shape
    return pl.pallas_call(
        sum_kernel,
        out_shape=jax.ShapeDtypeStruct(
            (expo_count, galaxy_count * rows // expo_count, coeff_dim), jnp.float32
        ),
        in_specs=[pl.BlockSpec(memory_space=pltpu.SMEM), whole_vmem()],
        out_specs=whole_vmem(),
        scratch_shapes=[pltpu.VMEM((galaxy_count + 8, rows, coeff_dim), jnp.float32)],
        compiler_params=pltpu.CompilerParams(vmem_limit_bytes=VMEM_BYTES),
        cost_estimate=pl.CostEstimate(flops=10**6, bytes_accessed=3 * 10**6, transcendentals=0),
        name="sum_galaxies",
    )(listed, back)


def exact_dot(a, b):
    return jnp.dot(a, b, precision=lax.Precision.HIGHEST)


def per_device(samples, basis, operators, cutouts, pixel_weights, detections, intersections):
    galaxy_count, sample_count, coeff_dim = samples.shape
    sky_count, expo_count = lax.axis_size("sky"), lax.axis_size("expo")
    send_cap = detections.shape[3]
    slots = sky_count * send_cap
    part = sample_count // expo_count // CHUNKS
    listed = detections.reshape(slots)
    flat_samples = samples.reshape(galaxy_count * sample_count, coeff_dim)

    def swap(values, axis_name, count):
        shape = values.shape
        values = values.reshape(count, shape[0] // count, *shape[1:])
        values = lax.all_to_all(values, axis_name, split_axis=0, concat_axis=0, tiled=True)
        return values.reshape(shape)

    grads, likes = [], []
    for chunk in range(CHUNKS):
        outgoing = gather_slots(chunk, expo_count, listed, flat_samples, galaxy_count)
        incoming = swap(outgoing, "sky", sky_count)
        slot_grads, pair_like = pair_terms(
            intersections, incoming, basis, operators, cutouts, pixel_weights
        )
        back = swap(slot_grads, "sky", sky_count)
        summed = sum_galaxies(listed, back, galaxy_count, expo_count)
        summed = lax.psum_scatter(summed, "expo", scatter_dimension=0, tiled=True)
        grads.append(summed.reshape(galaxy_count, part, coeff_dim))
        likes.append(pair_like.reshape(-1, expo_count, part))

    pair_like = jnp.stack(likes, axis=2).reshape(-1, sample_count)
    holds = intersections.reshape(1, -1) == jnp.arange(slots, dtype=jnp.int32)[:, None]
    back_like = swap(exact_dot(holds.astype(jnp.float32), pair_like), "sky", sky_count)
    owns = listed[None, :] == jnp.arange(galaxy_count, dtype=jnp.int32)[:, None]
    like_part = exact_dot(owns.astype(jnp.float32), back_like)
    like_part = like_part.reshape(galaxy_count, expo_count, -1).transpose(1, 0, 2)
    like_out = jnp.sum(lax.all_to_all(like_part, "expo", split_axis=0, concat_axis=0), axis=0)
    return like_out, jnp.concatenate(grads, axis=1)


def solution(mesh):
    placed = (
        P("sky", None, None),
        P(),
        P(("expo", "sky"), None, None),
        P(("expo", "sky"), None, None),
        P(("expo", "sky"), None, None),
        P("expo", "sky", None, None),
        P(("expo", "sky"), None),
    )
    return jax.shard_map(
        per_device,
        mesh=mesh,
        in_specs=placed,
        out_specs=(P("sky", "expo"), P("sky", "expo", None)),
        check_vma=False,
    )
```

time: 271 us -> 187 us (0.69)
  waiting for transfers between devices: 124 us -> 40.9 us
  matrix products: 55 us -> 0.4 us
  blocking collectives: 21.1 us -> 67.1 us
  Pallas kernels: 0 us -> 43.5 us
  local copies, waits for them, and re-layouts: 33.4 us -> 9.72 us
  starting transfers between devices: 13.7 us -> 7.38 us
  other arithmetic: 7.72 us -> 2.89 us
    all_to_all x3 -> x2, waiting for transfers between devices: 112 us -> 36.6 us  [swap(): lax.all_to_all(values, axis_name, split_axis=0, concat_axis=0, tiled=True)]
    all_to_all x0 -> x4, blocking collectives: none -> 67.1 us  [the longest x3 56.7 us: swap(): lax.all_to_all(values, axis_name, split_axis=0, concat_axis=0, tiled=True)]
    dot_general x6 -> x2, matrix products: 55 us -> 0.4 us  [exact_dot(): return jnp.dot(a, b, precision=lax.Precision.HIGHEST)]
    pallas_call x0 -> x6, Pallas kernels: none -> 43.5 us  [the longest x2 34.2 us: pair_terms(): pl.pallas_call(pair_kernel, grid_spec=pltpu.PrefetchScalarGridSpec(num_sc...]
    unnamed x1 -> x0, blocking collectives: 21.1 us -> none
    gather x2 -> x0, local copies, waits for them, and re-layouts: 10.3 us -> none  [the longest x1 6.06 us: per_device(): jnp.take(incoming, jnp.maximum(intersections, 0), axis=0)]
    scatter x2 -> x0, local copies, waits for them, and re-layouts: 8.4 us -> none  [the longest x1 7.5 us: per_device(): slot_grads.at[target]]
    reduce_scatter x1 -> x2, waiting for transfers between devices: 11.5 us -> 4.36 us  [per_device(): summed = lax.psum_scatter(summed, 'expo', scatter_dimension=0, tiled=True)]
  transfers between devices with their start and end apart: 4 -> 4, of which waited for: 4 -> 3; matrix products, arithmetic and copies ran while one was open for 2% -> 3% of each run, Pallas kernels for 0% -> 14%
where the time goes in v1:
time: 187 us; the launch traced here: 186 us
  blocking collectives  67.1 us (36%)
  Pallas kernels  43.5 us (23%)
  waiting for transfers between devices  40.9 us (22%)
  between operations  14.2 us (8%)
  local copies, waits for them, and re-layouts  9.72 us (5%)
  starting transfers between devices  7.38 us (4%)
  other arithmetic  2.89 us (2%)
    all_to_all x3, blocking collectives, swap(): lax.all_to_all(values, axis_name, split_axis=0, concat_axis=0, tiled=True)  56.7 us
    all_to_all x2, waiting for transfers between devices, swap(): lax.all_to_all(values, axis_name, split_axis=0, concat_axis=0, tiled=True)  36.6 us
    pallas_call x2, Pallas kernels, pair_terms(): pl.pallas_call(pair_kernel, grid_spec=pltpu.PrefetchScalarGridSpec(num_sc...  34.2 us
    all_to_all x1, blocking collectives, per_device(): lax.all_to_all(like_part, 'expo', split_axis=0, concat_axis=0)  10.4 us
    all_to_all x2, starting transfers between devices, swap(): lax.all_to_all(values, axis_name, split_axis=0, concat_axis=0, tiled=True)  7.29 us
    unnamed x24, local copies, waits for them, and re-layouts  5.9 us
    pallas_call x2, Pallas kernels, sum_galaxies(): pl.pallas_call(sum_kernel, out_shape=jax.ShapeDtypeStruct((expo_count, ga...  5.61 us
    reduce_scatter x2, waiting for transfers between devices, per_device(): summed = lax.psum_scatter(summed, 'expo', scatter_dimension=0, tiled=True)  4.36 us
  transfers between devices with their start and end apart: 4, of which 3 were waited for; matrix products, arithmetic and copies ran while one was open for 3% of the time, Pallas kernels for 14%

profile of v1, /device:TPU:0, one launch (start us, length us, event | category | flops | bytes accessed | tf_op | source)
XLA Modules:
  0.0 186.1 jit_solution(14817543693508630431)
XLA Ops:
  7.2 0.8 eq.41.listed_ref
  7.9 1.2 copy-done
  9.2 1.2 gather_slots.3
  10.5 26.1 %all_to_all.30 = bf16[8,24,16,256]{3,2,1,0:T(8,128)(2,1)S(1)} all-to-all(bf16[8,24,16,256]{3,2,1,0:T(8,128)(2,1)S(1)} %bitcast.42), channel_id=1, replica_groups=mesh['expo'=4,'sky'=8] {'sky'}, dimensions={0} | all-to-all | bytes 3145728 | tf_op jit(solution)/shard_map/all_to_all | solution.py:176
  36.6 17.1 %pair_terms.3 = (bf16[192,16,256]{2,1,0:T(8,128)(2,1)S(1)}, f32[8,16,16]{2,1,0:T(8,128)S(1)}) custom-call(s32[8,16]{1,0:T(8,128)S(1)} %copy-done.3, bf16[192,16,256]{2,1,0:T(8,128)(2,1)S(1)} %bitcast.47, bf16[256,1024]{1,0:T(8,128)(2,1)S(1)} %copy-done.4, bf16[8,1024,1024]{2,1,0:T(8,128)(2,1)} %op_ref.3, f32[8,16,1024]{2,1,0:T(8,128)S(1)} %copy-done.6, ...), custom_call_target="tpu_custom_call" | custom-call | flops 10737418240 | bytes 19922944 | tf_op jit(solution)/shard_map/pair_terms/pallas_call | solution.py:96
  53.7 1.1 copy-done.2
  54.8 3.7 %all-to-all-start.5 = ((bf16[8,24,16,256]{3,2,1,0:T(8,128)(2,1)}), bf16[8,24,16,256]{3,2,1,0:T(8,128)(2,1)S(1)}, u32[]{:S(2)}, u32[]{:S(2)}) async-start(bf16[8,24,16,256]{3,2,1,0:T(8,128)(2,1)} %bitcast.46), calls=%async_computation.6 | async-start | bytes 3145728 | tf_op jit(solution)/shard_map/all_to_all | solution.py:176
  58.6 2.4 %gather_slots.2 = bf16[192,16,256]{2,1,0:T(8,128)(2,1)} custom-call(s32[192]{0:T(256)S(1)} %eq.41.listed_ref, bf16[2048,256]{1,0:T(8,128)(2,1)S(1)} %bitcast.44), custom_call_target="tpu_custom_call" | custom-call | flops 100000000 | bytes 3000000 | tf_op jit(solution)/shard_map/gather_slots/pallas_call | solution.py:47
  61.0 18.5 %all-to-all-done.5 = bf16[8,24,16,256]{3,2,1,0:T(8,128)(2,1)S(1)} async-done(((bf16[8,24,16,256]{3,2,1,0:T(8,128)(2,1)}), bf16[8,24,16,256]{3,2,1,0:T(8,128)(2,1)S(1)}, u32[]{:S(2)}, u32[]{:S(2)}) %all-to-all-start.5) | async-done | bytes 1572896 | tf_op jit(solution)/shard_map/all_to_all | solution.py:176
  79.5 3.6 %all-to-all-start = ((bf16[8,24,16,256]{3,2,1,0:T(8,128)(2,1)}), bf16[8,24,16,256]{3,2,1,0:T(8,128)(2,1)S(1)}, u32[]{:S(2)}, u32[]{:S(2)}) async-start(bf16[8,24,16,256]{3,2,1,0:T(8,128)(2,1)} %bitcast.2), calls=%async_computation | async-start | bytes 3145728 | tf_op jit(solution)/shard_map/all_to_all | solution.py:176
  83.2 2.8 %sum_galaxies.3 = f32[4,256,256]{2,1,0:T(8,128)} custom-call(s32[192]{0:T(256)S(1)} %eq.41.listed_ref, bf16[192,16,256]{2,1,0:T(8,128)(2,1)S(1)} %bitcast.40), custom_call_target="tpu_custom_call" | custom-call | flops 1000000 | bytes 3000000 | tf_op jit(solution)/shard_map/sum_galaxies/pallas_call | solution.py:146
  86.0 18.0 %all-to-all-done = bf16[8,24,16,256]{3,2,1,0:T(8,128)(2,1)S(1)} async-done(((bf16[8,24,16,256]{3,2,1,0:T(8,128)(2,1)}), bf16[8,24,16,256]{3,2,1,0:T(8,128)(2,1)S(1)}, u32[]{:S(2)}, u32[]{:S(2)}) %all-to-all-start) | async-done | bytes 1572896 | tf_op jit(solution)/shard_map/all_to_all | solution.py:176
  104.1 1.0 copy-done.5
  105.1 1.0 copy-done.7
  106.2 1.0 copy-done.9
  107.2 17.1 %pair_terms.2 = (bf16[192,16,256]{2,1,0:T(8,128)(2,1)S(1)}, f32[8,16,16]{2,1,0:T(8,128)S(1)}) custom-call(s32[8,16]{1,0:T(8,128)S(1)} %copy-done.3, bf16[192,16,256]{2,1,0:T(8,128)(2,1)S(1)} %bitcast.45, bf16[256,1024]{1,0:T(8,128)(2,1)S(1)} %copy-done.5, bf16[8,1024,1024]{2,1,0:T(8,128)(2,1)} %op_ref.3, f32[8,16,1024]{2,1,0:T(8,128)S(1)} %copy-done.7, ...), custom_call_target="tpu_custom_call" | custom-call | flops 10737418240 | bytes 19922944 | tf_op jit(solution)/shard_map/pair_terms/pallas_call | solution.py:96
  124.3 23.4 %all_to_all.31 = bf16[8,24,16,256]{3,2,1,0:T(8,128)(2,1)S(1)} all-to-all(bf16[8,24,16,256]{3,2,1,0:T(8,128)(2,1)S(1)} %bitcast.48), channel_id=1, replica_groups=mesh['expo'=4,'sky'=8] {'sky'}, dimensions={0} | all-to-all | bytes 3145728 | tf_op jit(solution)/shard_map/all_to_all | solution.py:176
  147.7 2.8 %sum_galaxies.2 = f32[4,256,256]{2,1,0:T(8,128)} custom-call(s32[192]{0:T(256)S(1)} %eq.41.listed_ref, bf16[192,16,256]{2,1,0:T(8,128)(2,1)S(1)} %bitcast.41), custom_call_target="tpu_custom_call" | custom-call | flops 1000000 | bytes 3000000 | tf_op jit(solution)/shard_map/sum_galaxies/pallas_call | solution.py:146
  151.4 7.2 %all_to_all.32 = f32[8,1,768]{2,1,0:T(1,128)S(1)} all-to-all(f32[8,1,768]{2,1,0:T(1,128)S(1)} %reshape.83), channel_id=1, replica_groups=mesh['expo'=4,'sky'=8] {'sky'}, dimensions={0} | all-to-all | bytes 49152 | tf_op jit(solution)/shard_map/all_to_all | solution.py:176
  160.2 10.4 %all_to_all.33 = f32[4,1,512]{2,1,0:T(1,128)S(1)} all-to-all(f32[4,1,512]{2,1,0:T(1,128)S(1)} %reshape.85), channel_id=1, replica_groups=mesh['expo'=4,'sky'=8] {'expo'}, dimensions={0} | all-to-all | bytes 16384 | tf_op jit(solution)/shard_map/all_to_all | solution.py:198
  172.0 1.0 reshape.80
  173.0 4.4 %reduce-scatter.3.cloned.1.call-done = f32[1,256,256]{2,1,0:T(8,128)} async-done(((f32[4,256,256]{2,1,0:T(8,128)}), f32[1,256,256]{2,1,0:T(8,128)}) %reduce-scatter.3.cloned.1.call-update) | async-done | bytes 262160 | tf_op jit(solution)/shard_map/reduce_scatter | solution.py:188
  177.4 1.0 reshape.77
  178.4 0.9 pad_maximum_fusion
  (39 shorter events, 3.9 us)
Async XLA Ops:
  7.9 1.2 copy-start
  10.4 26.1 %copy-start.3 = (s32[8,16]{1,0:T(8,128)S(1)}, s32[8,16]{1,0:T(8,128)}, u32[]{:S(2)}) copy-start(s32[8,16]{1,0:T(8,128)} %inter_ref.3) | copy-start | bytes 1540
  10.4 26.1 %copy-start.4 = (bf16[256,1024]{1,0:T(8,128)(2,1)S(1)}, bf16[256,1024]{1,0:T(8,128)(2,1)}, u32[]{:S(2)}) copy-start(bf16[256,1024]{1,0:T(8,128)(2,1)} %basis_ref.3) | copy-start | bytes 1572868
  10.4 26.1 %copy-start.6 = (f32[8,16,1024]{2,1,0:T(8,128)S(1)}, f32[8,16,1024]{2,1,0:T(8,128)}, u32[]{:S(2)}) copy-start(f32[8,16,1024]{2,1,0:T(8,128)} %cut_ref.3) | copy-start | bytes 1572868
  10.4 26.1 %copy-start.8 = (f32[8,16,1024]{2,1,0:T(8,128)S(1)}, f32[8,16,1024]{2,1,0:T(8,128)}, u32[]{:S(2)}) copy-start(f32[8,16,1024]{2,1,0:T(8,128)} %weight_ref.3) | copy-start | bytes 1572868
  53.7 1.2 copy-start.2
  54.8 3.7 %copy-start.1 = (bf16[64,32,256]{2,1,0:T(8,128)(2,1)S(1)}, bf16[64,32,256]{2,1,0:T(8,128)(2,1)}, u32[]{:S(2)}) copy-start(bf16[64,32,256]{2,1,0:T(8,128)(2,1)} %param.7) | copy-start | bytes 3145732
  54.8 24.7 %all-to-all-start.5 = ((bf16[8,24,16,256]{3,2,1,0:T(8,128)(2,1)}), bf16[8,24,16,256]{3,2,1,0:T(8,128)(2,1)S(1)}, u32[]{:S(2)}, u32[]{:S(2)}) async-start(bf16[8,24,16,256]{3,2,1,0:T(8,128)(2,1)} %bitcast.46), calls=%async_computation.6 | async-start | bytes 3145728 | tf_op jit(solution)/shard_map/all_to_all | solution.py:176
  79.5 24.5 %all-to-all-start = ((bf16[8,24,16,256]{3,2,1,0:T(8,128)(2,1)}), bf16[8,24,16,256]{3,2,1,0:T(8,128)(2,1)S(1)}, u32[]{:S(2)}, u32[]{:S(2)}) async-start(bf16[8,24,16,256]{3,2,1,0:T(8,128)(2,1)} %bitcast.2), calls=%async_computation | async-start | bytes 3145728 | tf_op jit(solution)/shard_map/all_to_all | solution.py:176
  83.1 88.9 %reduce-scatter.5.cloned.1.call-start = ((), (), s32[]{:S(2)}) async-start(), calls=%async_computation.9 | async-start | bytes 1310720 | tf_op jit(solution)/shard_map/reduce_scatter | solution.py:188
  86.0 91.4 %reduce-scatter.3.cloned.1.call-start = ((), (), s32[]{:S(2)}) async-start(), calls=%async_computation.8 | async-start | bytes 1310720 | tf_op jit(solution)/shard_map/reduce_scatter | solution.py:188
  104.1 1.0 copy-start.5
  105.1 1.0 copy-start.7
  106.2 1.0 copy-start.9
Sparse Core Ops, SparseCore 0:
  86.2 28.7 reduce-scatter.4
  150.7 26.6 reduce-scatter.2

commit v2 on v1

--- a/solution.py
+++ b/solution.py
@@ -138,15 +138,15 @@
 
     for e in range(expo_count):
         mine = total[:galaxy_count, e * part : (e + 1) * part, :]
-        out_ref[e] = mine.reshape(galaxy_count * part, coeff_dim)
-
-
-def sum_galaxies(listed, back, galaxy_count, expo_count):
+        out_ref[e] = mine.reshape(galaxy_count * part, coeff_dim).astype(out_ref.dtype)
+
+
+def sum_galaxies(listed, back, galaxy_count, expo_count, kept):
     slots, rows, coeff_dim = back.shape
     return pl.pallas_call(
         sum_kernel,
         out_shape=jax.ShapeDtypeStruct(
-            (expo_count, galaxy_count * rows // expo_count, coeff_dim), jnp.float32
+            (expo_count, galaxy_count * rows // expo_count, coeff_dim), kept
         ),
         in_specs=[pl.BlockSpec(memory_space=pltpu.SMEM), whole_vmem()],
         out_specs=whole_vmem(),
@@ -176,18 +176,34 @@
         values = lax.all_to_all(values, axis_name, split_axis=0, concat_axis=0, tiled=True)
         return values.reshape(shape)
 
-    grads, likes = [], []
+    incoming = []
     for chunk in range(CHUNKS):
         outgoing = gather_slots(chunk, expo_count, listed, flat_samples, galaxy_count)
-        incoming = swap(outgoing, "sky", sky_count)
-        slot_grads, pair_like = pair_terms(
-            intersections, incoming, basis, operators, cutouts, pixel_weights
+        incoming.append(swap(outgoing, "sky", sky_count))
+    slot_grads, likes, grads = [], [], []
+    for chunk in range(CHUNKS):
+        pair_grads, pair_like = pair_terms(
+            intersections, incoming[chunk], basis, operators, cutouts, pixel_weights
         )
-        back = swap(slot_grads, "sky", sky_count)
-        summed = sum_galaxies(listed, back, galaxy_count, expo_count)
-        summed = lax.psum_scatter(summed, "expo", scatter_dimension=0, tiled=True)
+        if chunk + 1 < CHUNKS:
+            pair_grads, incoming[chunk + 1] = lax.optimization_barrier(
+                (pair_grads, incoming[chunk + 1])
+            )
+        slot_grads.append(pair_grads)
+        likes.append(pair_like.reshape(-1, expo_count, part))
+    for chunk in range(CHUNKS):
+        back = swap(slot_grads[chunk], "sky", sky_count)
+        last = chunk + 1 == CHUNKS
+        if not last:
+            back, slot_grads[chunk + 1] = lax.optimization_barrier((back, slot_grads[chunk + 1]))
+        kept = jnp.bfloat16 if last else jnp.float32
+        summed = sum_galaxies(listed, back, galaxy_count, expo_count, kept)
+        if last:
+            summed = lax.all_to_all(summed, "expo", split_axis=0, concat_axis=0, tiled=True)
+            summed = jnp.sum(summed.astype(jnp.float32), axis=0)
+        else:
+            summed = lax.psum_scatter(summed, "expo", scatter_dimension=0, tiled=True)
         grads.append(summed.reshape(galaxy_count, part, coeff_dim))
-        likes.append(pair_like.reshape(-1, expo_count, part))
 
     pair_like = jnp.stack(likes, axis=2).reshape(-1, sample_count)
     holds = intersections.reshape(1, -1) == jnp.arange(slots, dtype=jnp.int32)[:, None]

time: 187 us -> 159 us (0.85)
  blocking collectives: 67.1 us -> 0 us
  starting transfers between devices: 7.38 us -> 29.3 us
  waiting for transfers between devices: 40.9 us -> 50.5 us
  local copies, waits for them, and re-layouts: 9.72 us -> 15.2 us
    all_to_all x4 -> x0, blocking collectives: 67.1 us -> none  [the longest x3 56.7 us: swap(): lax.all_to_all(values, axis_name, split_axis=0, concat_axis=0, tiled=True)]
    all_to_all x2 -> x5, starting transfers between devices: 7.29 us -> 20.9 us  [swap(): lax.all_to_all(values, axis_name, split_axis=0, concat_axis=0, tiled=True)]
    all_to_all x0 -> x2, waiting for transfers between devices: none -> 11.3 us  [the longest x1 8.16 us: per_device(): lax.all_to_all(summed, 'expo', split_axis=0, concat_axis=0, tiled=True)]
    all_to_all x0 -> x2, starting transfers between devices: none -> 8.33 us  [the longest x1 4.86 us: per_device(): lax.all_to_all(like_part, 'expo', split_axis=0, concat_axis=0)]
    unnamed x24 -> x30, local copies, waits for them, and re-layouts: 5.9 us -> 12.3 us
    reduce_scatter x2 -> x1, waiting for transfers between devices: 4.36 us -> 0.01 us  [per_device(): summed = lax.psum_scatter(summed, 'expo', scatter_dimension=0, tiled=True)]
    all_to_all x2 -> x5, waiting for transfers between devices: 36.6 us -> 39.2 us  [swap(): lax.all_to_all(values, axis_name, split_axis=0, concat_axis=0, tiled=True)]
  transfers between devices with their start and end apart: 4 -> 8, of which waited for: 3 -> 5; matrix products, arithmetic and copies ran while one was open for 3% -> 4% of each run, Pallas kernels for 14% -> 27%
where the time goes in v2:
time: 159 us; the launch traced here: 157 us
  waiting for transfers between devices  50.5 us (32%)
  Pallas kernels  44.5 us (28%)
  starting transfers between devices  29.3 us (18%)
  local copies, waits for them, and re-layouts  15.2 us (10%)
  between operations  14.2 us (9%)
  other arithmetic  2.96 us (2%)
    all_to_all x5, waiting for transfers between devices, swap(): lax.all_to_all(values, axis_name, split_axis=0, concat_axis=0, tiled=True)  39.2 us
    pallas_call x2, Pallas kernels, pair_terms(): pl.pallas_call(pair_kernel, grid_spec=pltpu.PrefetchScalarGridSpec(num_sc...  35.3 us
    all_to_all x5, starting transfers between devices, swap(): lax.all_to_all(values, axis_name, split_axis=0, concat_axis=0, tiled=True)  20.9 us
    unnamed x30, local copies, waits for them, and re-layouts  12.3 us
    all_to_all x1, waiting for transfers between devices, per_device(): lax.all_to_all(summed, 'expo', split_axis=0, concat_axis=0, tiled=True)  8.16 us
    all_to_all x1, starting transfers between devices, per_device(): lax.all_to_all(like_part, 'expo', split_axis=0, concat_axis=0)  4.86 us
    pallas_call x2, Pallas kernels, gather_slots(): pl.pallas_call(functools.partial(gather_kernel, chunk, expo_count), out_s...  4.83 us
    pallas_call x2, Pallas kernels, sum_galaxies(): pl.pallas_call(sum_kernel, out_shape=jax.ShapeDtypeStruct((expo_count, ga...  4.41 us
  transfers between devices with their start and end apart: 8, of which 5 were waited for; matrix products, arithmetic and copies ran while one was open for 4% of the time, Pallas kernels for 27%

profile of v2, /device:TPU:0, one launch (start us, length us, event | category | flops | bytes accessed | tf_op | source)
XLA Modules:
  0.0 157.1 jit_solution(2436746996351790629)
XLA Ops:
  7.9 1.2 copy-done
  9.2 2.4 %gather_slots.2 = bf16[192,16,256]{2,1,0:T(8,128)(2,1)} custom-call(s32[192]{0:T(256)S(1)} %eq.41.listed_ref, bf16[2048,256]{1,0:T(8,128)(2,1)S(1)} %bitcast.42), custom_call_target="tpu_custom_call" | custom-call | flops 100000000 | bytes 3000000 | tf_op jit(solution)/shard_map/gather_slots/pallas_call | solution.py:47
  11.6 5.3 %all-to-all-start = ((bf16[8,24,16,256]{3,2,1,0:T(8,128)(2,1)}), bf16[8,24,16,256]{3,2,1,0:T(8,128)(2,1)S(1)}, u32[]{:S(2)}, u32[]{:S(2)}) async-start(bf16[8,24,16,256]{3,2,1,0:T(8,128)(2,1)} %bitcast.2), calls=%async_computation | async-start | bytes 3145728 | tf_op jit(solution)/shard_map/all_to_all | solution.py:176
  16.9 2.4 %gather_slots.3 = bf16[192,16,256]{2,1,0:T(8,128)(2,1)} custom-call(s32[192]{0:T(256)S(1)} %eq.41.listed_ref, bf16[2048,256]{1,0:T(8,128)(2,1)S(1)} %bitcast.43), custom_call_target="tpu_custom_call" | custom-call | flops 100000000 | bytes 3000000 | tf_op jit(solution)/shard_map/gather_slots/pallas_call | solution.py:47
  19.3 18.6 %all-to-all-done = bf16[8,24,16,256]{3,2,1,0:T(8,128)(2,1)S(1)} async-done(((bf16[8,24,16,256]{3,2,1,0:T(8,128)(2,1)}), bf16[8,24,16,256]{3,2,1,0:T(8,128)(2,1)S(1)}, u32[]{:S(2)}, u32[]{:S(2)}) %all-to-all-start) | async-done | bytes 1572896 | tf_op jit(solution)/shard_map/all_to_all | solution.py:176
  37.9 1.1 copy-done.4
  39.0 3.7 %all-to-all-start.1 = ((bf16[8,24,16,256]{3,2,1,0:T(8,128)(2,1)}), bf16[8,24,16,256]{3,2,1,0:T(8,128)(2,1)S(1)}, u32[]{:S(2)}, u32[]{:S(2)}) async-start(bf16[8,24,16,256]{3,2,1,0:T(8,128)(2,1)} %bitcast.4), calls=%async_computation.1 | async-start | bytes 3145728 | tf_op jit(solution)/shard_map/all_to_all | solution.py:176
  43.8 1.0 copy-done.9
  44.9 1.0 copy-done.11
  45.9 18.2 %pair_terms.2 = (bf16[192,16,256]{2,1,0:T(8,128)(2,1)}, f32[8,16,16]{2,1,0:T(8,128)S(1)}) custom-call(s32[8,16]{1,0:T(8,128)S(1)} %copy-done.6, bf16[192,16,256]{2,1,0:T(8,128)(2,1)S(1)} %bitcast.46, bf16[256,1024]{1,0:T(8,128)(2,1)S(1)} %copy-done.7, bf16[8,1024,1024]{2,1,0:T(8,128)(2,1)} %op_ref.3, f32[8,16,1024]{2,1,0:T(8,128)S(1)} %copy-done.9, ...), custom_call_target="tpu_custom_call" | custom-call | flops 10737418240 | bytes 19922944 | tf_op jit(solution)/shard_map/pair_terms/pallas_call | solution.py:96
  64.1 4.1 %all-to-all-start.4 = ((bf16[8,24,16,256]{3,2,1,0:T(8,128)(2,1)}), bf16[8,24,16,256]{3,2,1,0:T(8,128)(2,1)S(1)}, u32[]{:S(2)}, u32[]{:S(2)}) async-start(bf16[8,24,16,256]{3,2,1,0:T(8,128)(2,1)} %bitcast.12), calls=%async_computation.4 | async-start | bytes 3145728 | tf_op jit(solution)/shard_map/all_to_all | solution.py:176
  69.5 1.0 copy-done.10
  71.6 17.1 %pair_terms.3 = (bf16[192,16,256]{2,1,0:T(8,128)(2,1)S(1)}, f32[8,16,16]{2,1,0:T(8,128)S(1)}) custom-call(s32[8,16]{1,0:T(8,128)S(1)} %copy-done.6, bf16[192,16,256]{2,1,0:T(8,128)(2,1)S(1)} %bitcast.45, bf16[256,1024]{1,0:T(8,128)(2,1)S(1)} %copy-done.8, bf16[8,1024,1024]{2,1,0:T(8,128)(2,1)} %op_ref.3, f32[8,16,1024]{2,1,0:T(8,128)S(1)} %copy-done.10, ...), custom_call_target="tpu_custom_call" | custom-call | flops 10737418240 | bytes 19922944 | tf_op jit(solution)/shard_map/pair_terms/pallas_call | solution.py:96
  88.8 1.2 copy-done.3
  91.1 4.2 %all-to-all-start.2 = ((f32[8,1,768]{2,1,0:T(1,128)}), f32[8,1,768]{2,1,0:T(1,128)S(1)}, u32[]{:S(2)}, u32[]{:S(2)}) async-start(f32[8,1,768]{2,1,0:T(1,128)} %reshape.83), calls=%async_computation.2 | async-start | bytes 49152 | tf_op jit(solution)/shard_map/all_to_all | solution.py:176
  95.3 4.8 %all-to-all-done.2 = f32[8,1,768]{2,1,0:T(1,128)S(1)} async-done(((f32[8,1,768]{2,1,0:T(1,128)}), f32[8,1,768]{2,1,0:T(1,128)S(1)}, u32[]{:S(2)}, u32[]{:S(2)}) %all-to-all-start.2) | async-done | bytes 24608 | tf_op jit(solution)/shard_map/all_to_all | solution.py:176
  100.1 3.6 %all-to-all-start.5 = ((bf16[8,24,16,256]{3,2,1,0:T(8,128)(2,1)}), bf16[8,24,16,256]{3,2,1,0:T(8,128)(2,1)S(1)}, u32[]{:S(2)}, u32[]{:S(2)}) async-start(bf16[8,24,16,256]{3,2,1,0:T(8,128)(2,1)} %bitcast.44), calls=%async_computation.6 | async-start | bytes 3145728 | tf_op jit(solution)/shard_map/all_to_all | solution.py:176
  103.7 1.8 %sum_galaxies.2 = f32[4,256,256]{2,1,0:T(8,128)S(1)} custom-call(s32[192]{0:T(256)S(1)} %eq.41.listed_ref, bf16[192,16,256]{2,1,0:T(8,128)(2,1)S(1)} %bitcast.40), custom_call_target="tpu_custom_call" | custom-call | flops 1000000 | bytes 3000000 | tf_op jit(solution)/shard_map/sum_galaxies/pallas_call | solution.py:146
  108.8 15.8 %all-to-all-done.5 = bf16[8,24,16,256]{3,2,1,0:T(8,128)(2,1)S(1)} async-done(((bf16[8,24,16,256]{3,2,1,0:T(8,128)(2,1)}), bf16[8,24,16,256]{3,2,1,0:T(8,128)(2,1)S(1)}, u32[]{:S(2)}, u32[]{:S(2)}) %all-to-all-start.5) | async-done | bytes 1572896 | tf_op jit(solution)/shard_map/all_to_all | solution.py:176
  124.6 4.9 %all-to-all-start.3 = ((f32[4,1,512]{2,1,0:T(1,128)}), f32[4,1,512]{2,1,0:T(1,128)S(1)}, u32[]{:S(2)}, u32[]{:S(2)}) async-start(f32[4,1,512]{2,1,0:T(1,128)} %reshape.85), calls=%async_computation.3 | async-start | bytes 16384 | tf_op jit(solution)/shard_map/all_to_all | solution.py:214
  129.5 2.6 %sum_galaxies.3 = bf16[4,256,256]{2,1,0:T(8,128)(2,1)} custom-call(s32[192]{0:T(256)S(1)} %eq.41.listed_ref, bf16[192,16,256]{2,1,0:T(8,128)(2,1)S(1)} %bitcast.41), custom_call_target="tpu_custom_call" | custom-call | flops 1000000 | bytes 3000000 | tf_op jit(solution)/shard_map/sum_galaxies/pallas_call | solution.py:146
  132.1 3.1 %all-to-all-done.3 = f32[4,1,512]{2,1,0:T(1,128)S(1)} async-done(((f32[4,1,512]{2,1,0:T(1,128)}), f32[4,1,512]{2,1,0:T(1,128)S(1)}, u32[]{:S(2)}, u32[]{:S(2)}) %all-to-all-start.3) | async-done | bytes 8224 | tf_op jit(solution)/shard_map/all_to_all | solution.py:214
  135.2 3.5 %all-to-all-start.6 = ((bf16[4,256,256]{2,1,0:T(8,128)(2,1)}), bf16[4,256,256]{2,1,0:T(8,128)(2,1)S(1)}, u32[]{:S(2)}, u32[]{:S(2)}) async-start(bf16[4,256,256]{2,1,0:T(8,128)(2,1)} %sum_galaxies.3), calls=%async_computation.7 | async-start | bytes 1048576 | tf_op jit(solution)/shard_map/all_to_all | solution.py:202
  141.1 8.2 %all-to-all-done.6 = bf16[4,256,256]{2,1,0:T(8,128)(2,1)S(1)} async-done(((bf16[4,256,256]{2,1,0:T(8,128)(2,1)}), bf16[4,256,256]{2,1,0:T(8,128)(2,1)S(1)}, u32[]{:S(2)}, u32[]{:S(2)}) %all-to-all-start.6) | async-done | bytes 524320 | tf_op jit(solution)/shard_map/all_to_all | solution.py:202
  (49 shorter events, 12.0 us)
Async XLA Ops:
  7.9 1.2 copy-start
  11.6 5.3 %copy-start.1 = (bf16[64,32,256]{2,1,0:T(8,128)(2,1)S(1)}, bf16[64,32,256]{2,1,0:T(8,128)(2,1)}, u32[]{:S(2)}) copy-start(bf16[64,32,256]{2,1,0:T(8,128)(2,1)} %param.7) | copy-start | bytes 3145732
  11.6 26.3 %all-to-all-start = ((bf16[8,24,16,256]{3,2,1,0:T(8,128)(2,1)}), bf16[8,24,16,256]{3,2,1,0:T(8,128)(2,1)S(1)}, u32[]{:S(2)}, u32[]{:S(2)}) async-start(bf16[8,24,16,256]{3,2,1,0:T(8,128)(2,1)} %bitcast.2), calls=%async_computation | async-start | bytes 3145728 | tf_op jit(solution)/shard_map/all_to_all | solution.py:176
  37.9 1.1 copy-start.4
  39.0 3.7 %copy-start.5 = (bf16[8,24,16,256]{3,2,1,0:T(8,128)(2,1)S(1)}, bf16[8,24,16,256]{3,2,1,0:T(8,128)(2,1)}, u32[]{:S(2)}) copy-start(bf16[8,24,16,256]{3,2,1,0:T(8,128)(2,1)} %copy-done.4) | copy-start | bytes 4718596
  39.0 3.7 %copy-start.6 = (s32[8,16]{1,0:T(8,128)S(1)}, s32[8,16]{1,0:T(8,128)}, u32[]{:S(2)}) copy-start(s32[8,16]{1,0:T(8,128)} %inter_ref.3) | copy-start | bytes 1540
  39.0 25.1 %all-to-all-start.1 = ((bf16[8,24,16,256]{3,2,1,0:T(8,128)(2,1)}), bf16[8,24,16,256]{3,2,1,0:T(8,128)(2,1)S(1)}, u32[]{:S(2)}, u32[]{:S(2)}) async-start(bf16[8,24,16,256]{3,2,1,0:T(8,128)(2,1)} %bitcast.4), calls=%async_computation.1 | async-start | bytes 3145728 | tf_op jit(solution)/shard_map/all_to_all | solution.py:176
  42.8 1.0 copy-start.7
  43.8 1.0 copy-start.9
  44.9 1.0 copy-start.11
  64.1 27.0 %all-to-all-start.4 = ((bf16[8,24,16,256]{3,2,1,0:T(8,128)(2,1)}), bf16[8,24,16,256]{3,2,1,0:T(8,128)(2,1)S(1)}, u32[]{:S(2)}, u32[]{:S(2)}) async-start(bf16[8,24,16,256]{3,2,1,0:T(8,128)(2,1)} %bitcast.12), calls=%async_computation.4 | async-start | bytes 3145728 | tf_op jit(solution)/shard_map/all_to_all | solution.py:176
  68.5 1.0 copy-start.8
  69.5 1.0 copy-start.10
  70.6 1.0 copy-start.12
  88.7 1.2 copy-start.3
  91.1 9.0 %all-to-all-start.2 = ((f32[8,1,768]{2,1,0:T(1,128)}), f32[8,1,768]{2,1,0:T(1,128)S(1)}, u32[]{:S(2)}, u32[]{:S(2)}) async-start(f32[8,1,768]{2,1,0:T(1,128)} %reshape.83), calls=%async_computation.2 | async-start | bytes 49152 | tf_op jit(solution)/shard_map/all_to_all | solution.py:176
  100.1 24.5 %all-to-all-start.5 = ((bf16[8,24,16,256]{3,2,1,0:T(8,128)(2,1)}), bf16[8,24,16,256]{3,2,1,0:T(8,128)(2,1)S(1)}, u32[]{:S(2)}, u32[]{:S(2)}) async-start(bf16[8,24,16,256]{3,2,1,0:T(8,128)(2,1)} %bitcast.44), calls=%async_computation.6 | async-start | bytes 3145728 | tf_op jit(solution)/shard_map/all_to_all | solution.py:176
  103.7 36.4 %reduce-scatter.2.cloned.1.call-start = ((), (), s32[]{:S(2)}) async-start(), calls=%async_computation.8 | async-start | bytes 1310720 | tf_op jit(solution)/shard_map/reduce_scatter | solution.py:205
  105.5 1.0 copy-start.2
  124.6 10.6 %all-to-all-start.3 = ((f32[4,1,512]{2,1,0:T(1,128)}), f32[4,1,512]{2,1,0:T(1,128)S(1)}, u32[]{:S(2)}, u32[]{:S(2)}) async-start(f32[4,1,512]{2,1,0:T(1,128)} %reshape.85), calls=%async_computation.3 | async-start | bytes 16384 | tf_op jit(solution)/shard_map/all_to_all | solution.py:214
  135.2 14.0 %all-to-all-start.6 = ((bf16[4,256,256]{2,1,0:T(8,128)(2,1)}), bf16[4,256,256]{2,1,0:T(8,128)(2,1)S(1)}, u32[]{:S(2)}, u32[]{:S(2)}) async-start(bf16[4,256,256]{2,1,0:T(8,128)(2,1)} %sum_galaxies.3), calls=%async_computation.7 | async-start | bytes 1048576 | tf_op jit(solution)/shard_map/all_to_all | solution.py:202
Sparse Core Ops, SparseCore 0:
  106.8 28.8 reduce-scatter.1

commit v3 on v2

--- a/solution.py
+++ b/solution.py
@@ -9,6 +9,7 @@
 
 CHUNKS = 2
 VMEM_BYTES = 48 * 1024 * 1024
+PAIR_VMEM_BYTES = 60 * 1024 * 1024
 
 
 def whole_vmem():
@@ -115,7 +116,7 @@
             jax.ShapeDtypeStruct((slots, rows, coeff_dim), jnp.bfloat16),
             jax.ShapeDtypeStruct((tiles, cap, rows), jnp.float32),
         ],
-        compiler_params=pltpu.CompilerParams(vmem_limit_bytes=VMEM_BYTES),
+        compiler_params=pltpu.CompilerParams(vmem_limit_bytes=PAIR_VMEM_BYTES),
         cost_estimate=pl.CostEstimate(
             flops=flops, bytes_accessed=2 * operators.size + 4 * incoming.size, transcendentals=0
         ),
@@ -123,7 +124,8 @@
     )(intersections, incoming, basis, operators, cutouts, pixel_weights)
 
 
-def sum_kernel(listed_ref, back_ref, out_ref, total):
+def sum_kernel(listed_ref, back_ref, *refs):
+    *extra, out_ref, total = refs
     galaxy_count = total.shape[0] - 8
     expo_count = out_ref.shape[0]
     rows, coeff_dim = total.shape[1:]
@@ -138,23 +140,34 @@
 
     for e in range(expo_count):
         mine = total[:galaxy_count, e * part : (e + 1) * part, :]
-        out_ref[e] = mine.reshape(galaxy_count * part, coeff_dim).astype(out_ref.dtype)
-
-
-def sum_galaxies(listed, back, galaxy_count, expo_count, kept):
+        grad_rows = galaxy_count * part
+        out_ref[e, :grad_rows] = mine.reshape(grad_rows, coeff_dim).astype(out_ref.dtype)
+        for extra_ref in extra:
+            out_ref[e, grad_rows:] = extra_ref[e]
+
+
+def sum_galaxies(listed, back, galaxy_count, expo_count, kept, extra=()):
     slots, rows, coeff_dim = back.shape
+    out_rows = galaxy_count * rows // expo_count + sum(one.shape[1] for one in extra)
     return pl.pallas_call(
         sum_kernel,
-        out_shape=jax.ShapeDtypeStruct(
-            (expo_count, galaxy_count * rows // expo_count, coeff_dim), kept
-        ),
-        in_specs=[pl.BlockSpec(memory_space=pltpu.SMEM), whole_vmem()],
+        out_shape=jax.ShapeDtypeStruct((expo_count, out_rows, coeff_dim), kept),
+        in_specs=[pl.BlockSpec(memory_space=pltpu.SMEM)] + [whole_vmem()] * (1 + len(extra)),
         out_specs=whole_vmem(),
         scratch_shapes=[pltpu.VMEM((galaxy_count + 8, rows, coeff_dim), jnp.float32)],
         compiler_params=pltpu.CompilerParams(vmem_limit_bytes=VMEM_BYTES),
         cost_estimate=pl.CostEstimate(flops=10**6, bytes_accessed=3 * 10**6, transcendentals=0),
         name="sum_galaxies",
-    )(listed, back)
+    )(listed, back, *extra)
+
+
+def three_terms(values):
+    terms = []
+    for _ in range(3):
+        term = lax.reduce_precision(values, exponent_bits=8, mantissa_bits=7)
+        terms.append(term.astype(jnp.bfloat16))
+        values = values - term
+    return jnp.stack(terms)
 
 
 def exact_dot(a, b):
@@ -191,27 +204,38 @@
             )
         slot_grads.append(pair_grads)
         likes.append(pair_like.reshape(-1, expo_count, part))
+
+    share = sample_count // expo_count
+    pair_like = jnp.stack(likes, axis=2).reshape(-1, sample_count)
+    holds = intersections.reshape(1, -1) == jnp.arange(slots, dtype=jnp.int32)[:, None]
+    slot_like = exact_dot(holds.astype(jnp.float32), pair_like)
+    slot_like = slot_like.reshape(sky_count, send_cap * sample_count)
+    every_like = lax.all_gather(slot_like, "sky")
+    back_like = lax.dynamic_index_in_dim(every_like, lax.axis_index("sky"), 1, keepdims=False)
+    owns = listed[None, :] == jnp.arange(galaxy_count, dtype=jnp.int32)[:, None]
+    like_part = exact_dot(owns.astype(jnp.float32), back_like.reshape(slots, sample_count))
+    like_part = like_part.reshape(galaxy_count, expo_count, share).transpose(1, 0, 2)
+    packed = jnp.moveaxis(three_terms(like_part), 0, 1).reshape(expo_count, -1)
+    like_rows = -(-packed.shape[1] // (16 * coeff_dim)) * 16
+    used = packed.shape[1]
+    packed = jnp.pad(packed, ((0, 0), (0, like_rows * coeff_dim - used)))
+    packed = packed.reshape(expo_count, like_rows, coeff_dim)
+
     for chunk in range(CHUNKS):
         back = swap(slot_grads[chunk], "sky", sky_count)
-        last = chunk + 1 == CHUNKS
-        if not last:
+        if chunk + 1 < CHUNKS:
             back, slot_grads[chunk + 1] = lax.optimization_barrier((back, slot_grads[chunk + 1]))
-        kept = jnp.bfloat16 if last else jnp.float32
-        summed = sum_galaxies(listed, back, galaxy_count, expo_count, kept)
-        if last:
+            summed = sum_galaxies(listed, back, galaxy_count, expo_count, jnp.float32)
+            summed = lax.psum_scatter(summed, "expo", scatter_dimension=0, tiled=True)
+            grads.append(summed.reshape(galaxy_count, part, coeff_dim))
+        else:
+            summed = sum_galaxies(listed, back, galaxy_count, expo_count, jnp.bfloat16, (packed,))
             summed = lax.all_to_all(summed, "expo", split_axis=0, concat_axis=0, tiled=True)
-            summed = jnp.sum(summed.astype(jnp.float32), axis=0)
-        else:
-            summed = lax.psum_scatter(summed, "expo", scatter_dimension=0, tiled=True)
-        grads.append(summed.reshape(galaxy_count, part, coeff_dim))
-
-    pair_like = jnp.stack(likes, axis=2).reshape(-1, sample_count)
-    holds = intersections.reshape(1, -1) == jnp.arange(slots, dtype=jnp.int32)[:, None]
-    back_like = swap(exact_dot(holds.astype(jnp.float32), pair_like), "sky", sky_count)
-    owns = listed[None, :] == jnp.arange(galaxy_count, dtype=jnp.int32)[:, None]
-    like_part = exact_dot(owns.astype(jnp.float32), back_like)
-    like_part = like_part.reshape(galaxy_count, expo_count, -1).transpose(1, 0, 2)
-    like_out = jnp.sum(lax.all_to_all(like_part, "expo", split_axis=0, concat_axis=0), axis=0)
+            summed = summed.astype(jnp.float32)
+            mine = jnp.sum(summed[:, : galaxy_count * part], axis=0)
+            grads.append(mine.reshape(galaxy_count, part, coeff_dim))
+            terms = summed[:, galaxy_count * part :].reshape(expo_count, -1)[:, :used]
+            like_out = jnp.sum(terms.reshape(expo_count * 3, galaxy_count, share), axis=0)
     return like_out, jnp.concatenate(grads, axis=1)
 
 

time: 159 us -> 151 us (0.950)
  blocking collectives: 0 us -> 20.8 us
  waiting for transfers between devices: 50.5 us -> 38 us
  starting transfers between devices: 29.3 us -> 21 us
  local copies, waits for them, and re-layouts: 15.2 us -> 8.46 us
  Pallas kernels: 44.5 us -> 46.6 us
  other arithmetic: 2.96 us -> 1.11 us
    all_gather x0 -> x1, blocking collectives: none -> 20.8 us  [per_device(): every_like = lax.all_gather(slot_like, 'sky')]
    all_to_all x5 -> x4, waiting for transfers between devices: 39.2 us -> 23.3 us  [swap(): lax.all_to_all(values, axis_name, split_axis=0, concat_axis=0, tiled=True)]
    unnamed x30 -> x20, local copies, waits for them, and re-layouts: 12.3 us -> 5.23 us
    all_to_all x1, waiting for transfers between devices: 8.16 us -> 14.7 us  [per_device(): lax.all_to_all(summed, 'expo', split_axis=0, concat_axis=0, tiled=True)]
    all_to_all x5 -> x4, starting transfers between devices: 20.9 us -> 16 us  [swap(): lax.all_to_all(values, axis_name, split_axis=0, concat_axis=0, tiled=True)]
    all_to_all x1 -> x0, starting transfers between devices: 4.86 us -> none  [per_device(): lax.all_to_all(like_part, 'expo', split_axis=0, concat_axis=0)]
    all_to_all x1 -> x0, waiting for transfers between devices: 3.09 us -> none  [per_device(): lax.all_to_all(like_part, 'expo', split_axis=0, concat_axis=0)]
    pallas_call x2, Pallas kernels: 35.3 us -> 37.2 us  [pair_terms(): pl.pallas_call(pair_kernel, grid_spec=pltpu.PrefetchScalarGridSpec(num_sc...]
  transfers between devices with their start and end apart: 8 -> 6, of which waited for: 5 -> 4; matrix products, arithmetic and copies ran while one was open for 4% -> 2% of each run, Pallas kernels for 27% -> 29%
where the time goes in v3:
time: 151 us
  Pallas kernels  46.6 us (31%)
  waiting for transfers between devices  38 us (25%)
  starting transfers between devices  21 us (14%)
  blocking collectives  20.8 us (14%)
  between operations  14.3 us (9%)
  local copies, waits for them, and re-layouts  8.46 us (6%)
    pallas_call x2, Pallas kernels, pair_terms(): pl.pallas_call(pair_kernel, grid_spec=pltpu.PrefetchScalarGridSpec(num_sc...  37.2 us
    all_to_all x4, waiting for transfers between devices, swap(): lax.all_to_all(values, axis_name, split_axis=0, concat_axis=0, tiled=True)  23.3 us
    all_gather x1, blocking collectives, per_device(): every_like = lax.all_gather(slot_like, 'sky')  20.8 us
    all_to_all x4, starting transfers between devices, swap(): lax.all_to_all(values, axis_name, split_axis=0, concat_axis=0, tiled=True)  16 us
    all_to_all x1, waiting for transfers between devices, per_device(): lax.all_to_all(summed, 'expo', split_axis=0, concat_axis=0, tiled=True)  14.7 us
    unnamed x20, local copies, waits for them, and re-layouts  5.23 us
    all_to_all x1, starting transfers between devices, per_device(): lax.all_to_all(summed, 'expo', split_axis=0, concat_axis=0, tiled=True)  4.9 us
    pallas_call x2, Pallas kernels, gather_slots(): pl.pallas_call(functools.partial(gather_kernel, chunk, expo_count), out_s...  4.83 us
  transfers between devices with their start and end apart: 6, of which 4 were waited for; matrix products, arithmetic and copies ran while one was open for 2% of the time, Pallas kernels for 29%

profile of v3, /device:TPU:0, one launch (start us, length us, event | category | flops | bytes accessed | tf_op | source)
XLA Modules:
  0.0 150.5 jit_solution(2716466230296110602)
XLA Ops:
  7.2 0.8 reshape.64.listed_ref
  7.9 1.2 copy-done
  9.2 2.4 %gather_slots.2 = bf16[192,16,256]{2,1,0:T(8,128)(2,1)} custom-call(s32[192]{0:T(256)S(1)} %reshape.64.listed_ref, bf16[2048,256]{1,0:T(8,128)(2,1)S(1)} %bitcast.51), custom_call_target="tpu_custom_call" | custom-call | flops 100000000 | bytes 3000000 | tf_op jit(solution)/shard_map/gather_slots/pallas_call | solution.py:48
  11.6 5.3 %all-to-all-start = ((bf16[8,24,16,256]{3,2,1,0:T(8,128)(2,1)}), bf16[8,24,16,256]{3,2,1,0:T(8,128)(2,1)S(1)}, u32[]{:S(2)}, u32[]{:S(2)}) async-start(bf16[8,24,16,256]{3,2,1,0:T(8,128)(2,1)} %bitcast.1), calls=%async_computation | async-start | bytes 3145728 | tf_op jit(solution)/shard_map/all_to_all | solution.py:189
  16.9 2.4 %gather_slots.3 = bf16[192,16,256]{2,1,0:T(8,128)(2,1)} custom-call(s32[192]{0:T(256)S(1)} %reshape.64.listed_ref, bf16[2048,256]{1,0:T(8,128)(2,1)S(1)} %bitcast.52), custom_call_target="tpu_custom_call" | custom-call | flops 100000000 | bytes 3000000 | tf_op jit(solution)/shard_map/gather_slots/pallas_call | solution.py:48
  19.3 18.6 %all-to-all-done = bf16[8,24,16,256]{3,2,1,0:T(8,128)(2,1)S(1)} async-done(((bf16[8,24,16,256]{3,2,1,0:T(8,128)(2,1)}), bf16[8,24,16,256]{3,2,1,0:T(8,128)(2,1)S(1)}, u32[]{:S(2)}, u32[]{:S(2)}) %all-to-all-start) | async-done | bytes 1572896 | tf_op jit(solution)/shard_map/all_to_all | solution.py:189
  37.9 1.1 copy-done.4
  39.1 3.6 %all-to-all-start.1 = ((bf16[8,24,16,256]{3,2,1,0:T(8,128)(2,1)}), bf16[8,24,16,256]{3,2,1,0:T(8,128)(2,1)S(1)}, u32[]{:S(2)}, u32[]{:S(2)}) async-start(bf16[8,24,16,256]{3,2,1,0:T(8,128)(2,1)} %bitcast.3), calls=%async_computation.1 | async-start | bytes 3145728 | tf_op jit(solution)/shard_map/all_to_all | solution.py:189
  42.7 18.6 %pair_terms.2 = (bf16[192,16,256]{2,1,0:T(8,128)(2,1)}, f32[8,16,16]{2,1,0:T(8,128)}) custom-call(s32[8,16]{1,0:T(8,128)} %inter_ref.3, bf16[192,16,256]{2,1,0:T(8,128)(2,1)} %bitcast.56, bf16[256,1024]{1,0:T(8,128)(2,1)} %basis_ref.3, bf16[8,1024,1024]{2,1,0:T(8,128)(2,1)} %op_ref.3, f32[8,16,1024]{2,1,0:T(8,128)} %cut_ref.3, f32[8,16,1024]{2,1,0:T(8,128)} %weight_ref.3), custom_call_target="tpu_custom_call" | custom-call | flops 10737418240 | bytes 19922944 | tf_op jit(solution)/shard_map/pair_terms/pallas_call | solution.py:97
  61.3 2.3 %all-to-all-done.1 = bf16[8,24,16,256]{3,2,1,0:T(8,128)(2,1)S(1)} async-done(((bf16[8,24,16,256]{3,2,1,0:T(8,128)(2,1)}), bf16[8,24,16,256]{3,2,1,0:T(8,128)(2,1)S(1)}, u32[]{:S(2)}, u32[]{:S(2)}) %all-to-all-start.1) | async-done | bytes 1572896 | tf_op jit(solution)/shard_map/all_to_all | solution.py:189
  63.6 1.1 copy-done.3
  64.8 3.6 %all-to-all-start.2 = ((bf16[8,24,16,256]{3,2,1,0:T(8,128)(2,1)}), bf16[8,24,16,256]{3,2,1,0:T(8,128)(2,1)S(1)}, u32[]{:S(2)}, u32[]{:S(2)}) async-start(bf16[8,24,16,256]{3,2,1,0:T(8,128)(2,1)} %bitcast.57), calls=%async_computation.2 | async-start | bytes 3145728 | tf_op jit(solution)/shard_map/all_to_all | solution.py:189
  68.3 18.6 %pair_terms.3 = (bf16[192,16,256]{2,1,0:T(8,128)(2,1)}, f32[8,16,16]{2,1,0:T(8,128)}) custom-call(s32[8,16]{1,0:T(8,128)} %inter_ref.3, bf16[192,16,256]{2,1,0:T(8,128)(2,1)} %bitcast.55, bf16[256,1024]{1,0:T(8,128)(2,1)} %basis_ref.3, bf16[8,1024,1024]{2,1,0:T(8,128)(2,1)} %op_ref.3, f32[8,16,1024]{2,1,0:T(8,128)} %cut_ref.3, f32[8,16,1024]{2,1,0:T(8,128)} %weight_ref.3), custom_call_target="tpu_custom_call" | custom-call | flops 10737418240 | bytes 19922944 | tf_op jit(solution)/shard_map/pair_terms/pallas_call | solution.py:97
  86.9 2.4 %all-to-all-done.2 = bf16[8,24,16,256]{3,2,1,0:T(8,128)(2,1)S(1)} async-done(((bf16[8,24,16,256]{3,2,1,0:T(8,128)(2,1)}), bf16[8,24,16,256]{3,2,1,0:T(8,128)(2,1)S(1)}, u32[]{:S(2)}, u32[]{:S(2)}) %all-to-all-start.2) | async-done | bytes 1572896 | tf_op jit(solution)/shard_map/all_to_all | solution.py:189
  89.3 3.6 %all-to-all-start.3 = ((bf16[8,24,16,256]{3,2,1,0:T(8,128)(2,1)}), bf16[8,24,16,256]{3,2,1,0:T(8,128)(2,1)S(1)}, u32[]{:S(2)}, u32[]{:S(2)}) async-start(bf16[8,24,16,256]{3,2,1,0:T(8,128)(2,1)} %bitcast.54), calls=%async_computation.3 | async-start | bytes 3145728 | tf_op jit(solution)/shard_map/all_to_all | solution.py:189
  93.0 1.8 %sum_galaxies.3 = f32[4,256,256]{2,1,0:T(8,128)S(1)} custom-call(s32[192]{0:T(256)S(1)} %reshape.64.listed_ref, bf16[192,16,256]{2,1,0:T(8,128)(2,1)S(1)} %bitcast.49), custom_call_target="tpu_custom_call" | custom-call | flops 1000000 | bytes 3000000 | tf_op jit(solution)/shard_map/sum_galaxies/pallas_call | solution.py:152
  94.8 1.0 copy-done.2
  96.6 20.8 %all_gather.3 = f32[8,8,768]{2,1,0:T(8,128)S(1)} all-gather(f32[1,8,768]{2,1,0:T(8,128)S(1)} %all_gather_reshape.3), channel_id=1, replica_groups=mesh['expo'=4,'sky'=8] {'sky'}, dimensions={0}, use_global_device_ids=true | all-gather | bytes 221184 | tf_op jit(solution)/shard_map/all_gather | solution.py:213
  118.3 2.7 %sum_galaxies.2 = bf16[4,272,256]{2,1,0:T(8,128)(2,1)} custom-call(s32[192]{0:T(256)S(1)} %reshape.64.listed_ref, bf16[192,16,256]{2,1,0:T(8,128)(2,1)S(1)} %bitcast.50, bf16[4,16,256]{2,1,0:T(8,128)(2,1)S(1)} %bitcast.53), custom_call_target="tpu_custom_call" | custom-call | flops 1000000 | bytes 3000000 | tf_op jit(solution)/shard_map/sum_galaxies/pallas_call | solution.py:152
  120.9 4.9 %all-to-all-start.4 = ((bf16[4,272,256]{2,1,0:T(8,128)(2,1)}), bf16[4,272,256]{2,1,0:T(8,128)(2,1)S(1)}, u32[]{:S(2)}, u32[]{:S(2)}) async-start(bf16[4,272,256]{2,1,0:T(8,128)(2,1)} %sum_galaxies.2), calls=%async_computation.4 | async-start | bytes 1114112 | tf_op jit(solution)/shard_map/all_to_all | solution.py:233
  125.8 1.0 reshape.80
  126.9 14.7 %all-to-all-done.4 = bf16[4,272,256]{2,1,0:T(8,128)(2,1)S(1)} async-done(((bf16[4,272,256]{2,1,0:T(8,128)(2,1)}), bf16[4,272,256]{2,1,0:T(8,128)(2,1)S(1)}, u32[]{:S(2)}, u32[]{:S(2)}) %all-to-all-start.4) | async-done | bytes 557088 | tf_op jit(solution)/shard_map/all_to_all | solution.py:233
  142.1 0.7 copy.21
  142.8 0.9 pad_maximum_fusion
  (42 shorter events, 2.2 us)
Async XLA Ops:
  7.9 1.2 copy-start
  11.6 5.3 %copy-start.1 = (bf16[64,32,256]{2,1,0:T(8,128)(2,1)S(1)}, bf16[64,32,256]{2,1,0:T(8,128)(2,1)}, u32[]{:S(2)}) copy-start(bf16[64,32,256]{2,1,0:T(8,128)(2,1)} %param.7) | copy-start | bytes 3145732
  11.6 26.3 %all-to-all-start = ((bf16[8,24,16,256]{3,2,1,0:T(8,128)(2,1)}), bf16[8,24,16,256]{3,2,1,0:T(8,128)(2,1)S(1)}, u32[]{:S(2)}, u32[]{:S(2)}) async-start(bf16[8,24,16,256]{3,2,1,0:T(8,128)(2,1)} %bitcast.1), calls=%async_computation | async-start | bytes 3145728 | tf_op jit(solution)/shard_map/all_to_all | solution.py:189
  37.9 1.1 copy-start.4
  39.1 24.5 %all-to-all-start.1 = ((bf16[8,24,16,256]{3,2,1,0:T(8,128)(2,1)}), bf16[8,24,16,256]{3,2,1,0:T(8,128)(2,1)S(1)}, u32[]{:S(2)}, u32[]{:S(2)}) async-start(bf16[8,24,16,256]{3,2,1,0:T(8,128)(2,1)} %bitcast.3), calls=%async_computation.1 | async-start | bytes 3145728 | tf_op jit(solution)/shard_map/all_to_all | solution.py:189
  63.6 1.1 copy-start.3
  64.8 24.5 %all-to-all-start.2 = ((bf16[8,24,16,256]{3,2,1,0:T(8,128)(2,1)}), bf16[8,24,16,256]{3,2,1,0:T(8,128)(2,1)S(1)}, u32[]{:S(2)}, u32[]{:S(2)}) async-start(bf16[8,24,16,256]{3,2,1,0:T(8,128)(2,1)} %bitcast.57), calls=%async_computation.2 | async-start | bytes 3145728 | tf_op jit(solution)/shard_map/all_to_all | solution.py:189
  89.3 28.9 %all-to-all-start.3 = ((bf16[8,24,16,256]{3,2,1,0:T(8,128)(2,1)}), bf16[8,24,16,256]{3,2,1,0:T(8,128)(2,1)S(1)}, u32[]{:S(2)}, u32[]{:S(2)}) async-start(bf16[8,24,16,256]{3,2,1,0:T(8,128)(2,1)} %bitcast.54), calls=%async_computation.3 | async-start | bytes 3145728 | tf_op jit(solution)/shard_map/all_to_all | solution.py:189
  92.9 2.9 %copy-start.7 = (s32[8,16]{1,0:T(8,128)S(1)}, s32[8,16]{1,0:T(8,128)}, u32[]{:S(2)}) copy-start(s32[8,16]{1,0:T(8,128)} %inter_ref.3) | copy-start | bytes 1540
  92.9 3.0 %copy-start.5 = (f32[8,16,16]{2,1,0:T(8,128)S(1)}, f32[8,16,16]{2,1,0:T(8,128)}, u32[]{:S(2)}) copy-start(f32[8,16,16]{2,1,0:T(8,128)} %get-tuple-element.15) | copy-start | bytes 24580
  92.9 3.2 %copy-start.6 = (f32[8,16,16]{2,1,0:T(8,128)S(1)}, f32[8,16,16]{2,1,0:T(8,128)}, u32[]{:S(2)}) copy-start(f32[8,16,16]{2,1,0:T(8,128)} %get-tuple-element.16) | copy-start | bytes 24580
  92.9 32.9 %reduce-scatter.2.cloned.1.call-start = ((), (), s32[]{:S(2)}) async-start(), calls=%async_computation.6 | async-start | bytes 1310720 | tf_op jit(solution)/shard_map/reduce_scatter | solution.py:229
  94.8 1.0 copy-start.2
  120.9 20.6 %all-to-all-start.4 = ((bf16[4,272,256]{2,1,0:T(8,128)(2,1)}), bf16[4,272,256]{2,1,0:T(8,128)(2,1)S(1)}, u32[]{:S(2)}, u32[]{:S(2)}) async-start(bf16[4,272,256]{2,1,0:T(8,128)(2,1)} %sum_galaxies.2), calls=%async_computation.4 | async-start | bytes 1114112 | tf_op jit(solution)/shard_map/all_to_all | solution.py:233
Sparse Core Ops, SparseCore 0:
  96.1 28.7 reduce-scatter.1

commit v4 on v3

--- a/solution.py
+++ b/solution.py
@@ -210,8 +210,15 @@
     holds = intersections.reshape(1, -1) == jnp.arange(slots, dtype=jnp.int32)[:, None]
     slot_like = exact_dot(holds.astype(jnp.float32), pair_like)
     slot_like = slot_like.reshape(sky_count, send_cap * sample_count)
-    every_like = lax.all_gather(slot_like, "sky")
-    back_like = lax.dynamic_index_in_dim(every_like, lax.axis_index("sky"), 1, keepdims=False)
+    me = lax.axis_index("sky")
+    back_like = jnp.zeros_like(slot_like)
+    for shift in range(sky_count):
+        row = lax.dynamic_index_in_dim(slot_like, (me + shift) % sky_count, 0)
+        if shift:
+            pairs = [(c, (c + shift) % sky_count) for c in range(sky_count)]
+            row = lax.ppermute(row, "sky", pairs)
+        source = (me + sky_count - shift) % sky_count
+        back_like = lax.dynamic_update_index_in_dim(back_like, row, source, 0)
     owns = listed[None, :] == jnp.arange(galaxy_count, dtype=jnp.int32)[:, None]
     like_part = exact_dot(owns.astype(jnp.float32), back_like.reshape(slots, sample_count))
     like_part = like_part.reshape(galaxy_count, expo_count, share).transpose(1, 0, 2)

time: 151 us -> 151 us (level)
  blocking collectives: 20.8 us -> 0 us
  waiting for transfers between devices: 38 us -> 51.9 us
  starting transfers between devices: 21 us -> 27 us
    all_gather x1 -> x0, blocking collectives: 20.8 us -> none  [per_device(): every_like = lax.all_gather(slot_like, 'sky')]
    ppermute x0 -> x7, waiting for transfers between devices: none -> 14.1 us  [per_device(): row = lax.ppermute(row, 'sky', pairs)]
    ppermute x0 -> x7, starting transfers between devices: none -> 6.18 us  [per_device(): row = lax.ppermute(row, 'sky', pairs)]
  transfers between devices with their start and end apart: 6 -> 13, of which waited for: 4 -> 6; matrix products, arithmetic and copies ran while one was open for 2% -> 2% of each run, Pallas kernels for 29% -> 29%
where the time goes in v4:
time: 151 us
  waiting for transfers between devices  51.9 us (34%)
  Pallas kernels  46.6 us (31%)
  starting transfers between devices  27 us (18%)
  between operations  14.5 us (10%)
  local copies, waits for them, and re-layouts  9.09 us (6%)
    pallas_call x2, Pallas kernels, pair_terms(): pl.pallas_call(pair_kernel, grid_spec=pltpu.PrefetchScalarGridSpec(num_sc...  37.2 us
    all_to_all x4, waiting for transfers between devices, swap(): lax.all_to_all(values, axis_name, split_axis=0, concat_axis=0, tiled=True)  23.3 us
    all_to_all x4, starting transfers between devices, swap(): lax.all_to_all(values, axis_name, split_axis=0, concat_axis=0, tiled=True)  16 us
    all_to_all x1, waiting for transfers between devices, per_device(): lax.all_to_all(summed, 'expo', split_axis=0, concat_axis=0, tiled=True)  14.5 us
    ppermute x7, waiting for transfers between devices, per_device(): row = lax.ppermute(row, 'sky', pairs)  14.1 us
    ppermute x7, starting transfers between devices, per_device(): row = lax.ppermute(row, 'sky', pairs)  6.18 us
    unnamed x20, local copies, waits for them, and re-layouts  5.29 us
    pallas_call x2, Pallas kernels, gather_slots(): pl.pallas_call(functools.partial(gather_kernel, chunk, expo_count), out_s...  4.81 us
  transfers between devices with their start and end apart: 13, of which 6 were waited for; matrix products, arithmetic and copies ran while one was open for 2% of the time, Pallas kernels for 29%

profile of v4, /device:TPU:0, one launch (start us, length us, event | category | flops | bytes accessed | tf_op | source)
XLA Modules:
  0.0 150.6 jit_solution(18418918283928803818)
XLA Ops:
  7.9 1.2 copy-done
  9.2 2.4 %gather_slots.2 = bf16[192,16,256]{2,1,0:T(8,128)(2,1)} custom-call(s32[192]{0:T(256)S(1)} %reshape.66.listed_ref, bf16[2048,256]{1,0:T(8,128)(2,1)S(1)} %bitcast.51), custom_call_target="tpu_custom_call" | custom-call | flops 100000000 | bytes 3000000 | tf_op jit(solution)/shard_map/gather_slots/pallas_call | solution.py:48
  11.6 5.3 %all-to-all-start = ((bf16[8,24,16,256]{3,2,1,0:T(8,128)(2,1)}), bf16[8,24,16,256]{3,2,1,0:T(8,128)(2,1)S(1)}, u32[]{:S(2)}, u32[]{:S(2)}) async-start(bf16[8,24,16,256]{3,2,1,0:T(8,128)(2,1)} %bitcast.1), calls=%async_computation | async-start | bytes 3145728 | tf_op jit(solution)/shard_map/all_to_all | solution.py:189
  16.9 2.4 %gather_slots.3 = bf16[192,16,256]{2,1,0:T(8,128)(2,1)} custom-call(s32[192]{0:T(256)S(1)} %reshape.66.listed_ref, bf16[2048,256]{1,0:T(8,128)(2,1)S(1)} %bitcast.52), custom_call_target="tpu_custom_call" | custom-call | flops 100000000 | bytes 3000000 | tf_op jit(solution)/shard_map/gather_slots/pallas_call | solution.py:48
  19.3 18.6 %all-to-all-done = bf16[8,24,16,256]{3,2,1,0:T(8,128)(2,1)S(1)} async-done(((bf16[8,24,16,256]{3,2,1,0:T(8,128)(2,1)}), bf16[8,24,16,256]{3,2,1,0:T(8,128)(2,1)S(1)}, u32[]{:S(2)}, u32[]{:S(2)}) %all-to-all-start) | async-done | bytes 1572896 | tf_op jit(solution)/shard_map/all_to_all | solution.py:189
  37.9 1.2 copy-done.4
  39.1 3.6 %all-to-all-start.1 = ((bf16[8,24,16,256]{3,2,1,0:T(8,128)(2,1)}), bf16[8,24,16,256]{3,2,1,0:T(8,128)(2,1)S(1)}, u32[]{:S(2)}, u32[]{:S(2)}) async-start(bf16[8,24,16,256]{3,2,1,0:T(8,128)(2,1)} %bitcast.3), calls=%async_computation.1 | async-start | bytes 3145728 | tf_op jit(solution)/shard_map/all_to_all | solution.py:189
  42.7 18.6 %pair_terms.2 = (bf16[192,16,256]{2,1,0:T(8,128)(2,1)}, f32[8,16,16]{2,1,0:T(8,128)}) custom-call(s32[8,16]{1,0:T(8,128)} %inter_ref.3, bf16[192,16,256]{2,1,0:T(8,128)(2,1)} %bitcast.56, bf16[256,1024]{1,0:T(8,128)(2,1)} %basis_ref.3, bf16[8,1024,1024]{2,1,0:T(8,128)(2,1)} %op_ref.3, f32[8,16,1024]{2,1,0:T(8,128)} %cut_ref.3, f32[8,16,1024]{2,1,0:T(8,128)} %weight_ref.3), custom_call_target="tpu_custom_call" | custom-call | flops 10737418240 | bytes 19922944 | tf_op jit(solution)/shard_map/pair_terms/pallas_call | solution.py:97
  61.3 2.3 %all-to-all-done.1 = bf16[8,24,16,256]{3,2,1,0:T(8,128)(2,1)S(1)} async-done(((bf16[8,24,16,256]{3,2,1,0:T(8,128)(2,1)}), bf16[8,24,16,256]{3,2,1,0:T(8,128)(2,1)S(1)}, u32[]{:S(2)}, u32[]{:S(2)}) %all-to-all-start.1) | async-done | bytes 1572896 | tf_op jit(solution)/shard_map/all_to_all | solution.py:189
  63.6 1.2 copy-done.3
  64.8 3.6 %all-to-all-start.2 = ((bf16[8,24,16,256]{3,2,1,0:T(8,128)(2,1)}), bf16[8,24,16,256]{3,2,1,0:T(8,128)(2,1)S(1)}, u32[]{:S(2)}, u32[]{:S(2)}) async-start(bf16[8,24,16,256]{3,2,1,0:T(8,128)(2,1)} %bitcast.57), calls=%async_computation.2 | async-start | bytes 3145728 | tf_op jit(solution)/shard_map/all_to_all | solution.py:189
  68.4 18.6 %pair_terms.3 = (bf16[192,16,256]{2,1,0:T(8,128)(2,1)}, f32[8,16,16]{2,1,0:T(8,128)}) custom-call(s32[8,16]{1,0:T(8,128)} %inter_ref.3, bf16[192,16,256]{2,1,0:T(8,128)(2,1)} %bitcast.55, bf16[256,1024]{1,0:T(8,128)(2,1)} %basis_ref.3, bf16[8,1024,1024]{2,1,0:T(8,128)(2,1)} %op_ref.3, f32[8,16,1024]{2,1,0:T(8,128)} %cut_ref.3, f32[8,16,1024]{2,1,0:T(8,128)} %weight_ref.3), custom_call_target="tpu_custom_call" | custom-call | flops 10737418240 | bytes 19922944 | tf_op jit(solution)/shard_map/pair_terms/pallas_call | solution.py:97
  87.0 2.4 %all-to-all-done.2 = bf16[8,24,16,256]{3,2,1,0:T(8,128)(2,1)S(1)} async-done(((bf16[8,24,16,256]{3,2,1,0:T(8,128)(2,1)}), bf16[8,24,16,256]{3,2,1,0:T(8,128)(2,1)S(1)}, u32[]{:S(2)}, u32[]{:S(2)}) %all-to-all-start.2) | async-done | bytes 1572896 | tf_op jit(solution)/shard_map/all_to_all | solution.py:189
  89.3 3.6 %all-to-all-start.3 = ((bf16[8,24,16,256]{3,2,1,0:T(8,128)(2,1)}), bf16[8,24,16,256]{3,2,1,0:T(8,128)(2,1)S(1)}, u32[]{:S(2)}, u32[]{:S(2)}) async-start(bf16[8,24,16,256]{3,2,1,0:T(8,128)(2,1)} %bitcast.54), calls=%async_computation.3 | async-start | bytes 3145728 | tf_op jit(solution)/shard_map/all_to_all | solution.py:189
  93.0 1.9 %sum_galaxies.3 = f32[4,256,256]{2,1,0:T(8,128)S(1)} custom-call(s32[192]{0:T(256)S(1)} %reshape.66.listed_ref, bf16[192,16,256]{2,1,0:T(8,128)(2,1)S(1)} %bitcast.49), custom_call_target="tpu_custom_call" | custom-call | flops 1000000 | bytes 3000000 | tf_op jit(solution)/shard_map/sum_galaxies/pallas_call | solution.py:152
  96.8 1.8 %collective-permute-start.1 = (f32[1,768]{1,0:T(1,128)S(1)}, f32[1,768]{1,0:T(1,128)S(1)}, u32[]{:S(2)}, u32[]{:S(2)}) collective-permute-start(f32[1,768]{1,0:T(1,128)S(1)} %get-tuple-element.25), channel_id=1, source_target_pairs={{0,2},{1,3},{2,4},{3,5},{4,6},{5,7},{6,0},{7,1},{8,10},{9,11},{10,... | collective-permute-start | bytes 9224 | tf_op jit(solution)/shard_map/ppermute | solution.py:219
  98.6 1.4 collective-permute-start.4
  100.1 1.3 collective-permute-start.2
  102.0 12.0 %collective-permute-done.1 = f32[1,768]{1,0:T(1,128)S(1)} collective-permute-done((f32[1,768]{1,0:T(1,128)S(1)}, f32[1,768]{1,0:T(1,128)S(1)}, u32[]{:S(2)}, u32[]{:S(2)}) %collective-permute-start.1) | collective-permute-done | bytes 3104 | tf_op jit(solution)/shard_map/ppermute | solution.py:219
  115.6 2.0 %collective-permute-done.5 = f32[1,768]{1,0:T(1,128)S(1)} collective-permute-done((f32[1,768]{1,0:T(1,128)S(1)}, f32[1,768]{1,0:T(1,128)S(1)}, u32[]{:S(2)}, u32[]{:S(2)}) %collective-permute-start.5) | collective-permute-done | bytes 3104 | tf_op jit(solution)/shard_map/ppermute | solution.py:219
  118.6 2.7 %sum_galaxies.2 = bf16[4,272,256]{2,1,0:T(8,128)(2,1)} custom-call(s32[192]{0:T(256)S(1)} %reshape.66.listed_ref, bf16[192,16,256]{2,1,0:T(8,128)(2,1)S(1)} %bitcast.50, bf16[4,16,256]{2,1,0:T(8,128)(2,1)S(1)} %bitcast.53), custom_call_target="tpu_custom_call" | custom-call | flops 1000000 | bytes 3000000 | tf_op jit(solution)/shard_map/sum_galaxies/pallas_call | solution.py:152
  121.3 4.8 %all-to-all-start.4 = ((bf16[4,272,256]{2,1,0:T(8,128)(2,1)}), bf16[4,272,256]{2,1,0:T(8,128)(2,1)S(1)}, u32[]{:S(2)}, u32[]{:S(2)}) async-start(bf16[4,272,256]{2,1,0:T(8,128)(2,1)} %sum_galaxies.2), calls=%async_computation.4 | async-start | bytes 1114112 | tf_op jit(solution)/shard_map/all_to_all | solution.py:240
  126.0 1.0 reshape.83
  127.1 14.5 %all-to-all-done.4 = bf16[4,272,256]{2,1,0:T(8,128)(2,1)S(1)} async-done(((bf16[4,272,256]{2,1,0:T(8,128)(2,1)}), bf16[4,272,256]{2,1,0:T(8,128)(2,1)S(1)}, u32[]{:S(2)}, u32[]{:S(2)}) %all-to-all-start.4) | async-done | bytes 557088 | tf_op jit(solution)/shard_map/all_to_all | solution.py:240
  (64 shorter events, 7.7 us)
Async XLA Ops:
  7.9 1.2 copy-start
  11.6 5.3 %copy-start.1 = (bf16[64,32,256]{2,1,0:T(8,128)(2,1)S(1)}, bf16[64,32,256]{2,1,0:T(8,128)(2,1)}, u32[]{:S(2)}) copy-start(bf16[64,32,256]{2,1,0:T(8,128)(2,1)} %param.7) | copy-start | bytes 3145732
  11.6 26.3 %all-to-all-start = ((bf16[8,24,16,256]{3,2,1,0:T(8,128)(2,1)}), bf16[8,24,16,256]{3,2,1,0:T(8,128)(2,1)S(1)}, u32[]{:S(2)}, u32[]{:S(2)}) async-start(bf16[8,24,16,256]{3,2,1,0:T(8,128)(2,1)} %bitcast.1), calls=%async_computation | async-start | bytes 3145728 | tf_op jit(solution)/shard_map/all_to_all | solution.py:189
  37.9 1.2 copy-start.4
  39.1 24.5 %all-to-all-start.1 = ((bf16[8,24,16,256]{3,2,1,0:T(8,128)(2,1)}), bf16[8,24,16,256]{3,2,1,0:T(8,128)(2,1)S(1)}, u32[]{:S(2)}, u32[]{:S(2)}) async-start(bf16[8,24,16,256]{3,2,1,0:T(8,128)(2,1)} %bitcast.3), calls=%async_computation.1 | async-start | bytes 3145728 | tf_op jit(solution)/shard_map/all_to_all | solution.py:189
  63.6 1.2 copy-start.3
  64.8 24.5 %all-to-all-start.2 = ((bf16[8,24,16,256]{3,2,1,0:T(8,128)(2,1)}), bf16[8,24,16,256]{3,2,1,0:T(8,128)(2,1)S(1)}, u32[]{:S(2)}, u32[]{:S(2)}) async-start(bf16[8,24,16,256]{3,2,1,0:T(8,128)(2,1)} %bitcast.57), calls=%async_computation.2 | async-start | bytes 3145728 | tf_op jit(solution)/shard_map/all_to_all | solution.py:189
  89.3 29.2 %all-to-all-start.3 = ((bf16[8,24,16,256]{3,2,1,0:T(8,128)(2,1)}), bf16[8,24,16,256]{3,2,1,0:T(8,128)(2,1)S(1)}, u32[]{:S(2)}, u32[]{:S(2)}) async-start(bf16[8,24,16,256]{3,2,1,0:T(8,128)(2,1)} %bitcast.54), calls=%async_computation.3 | async-start | bytes 3145728 | tf_op jit(solution)/shard_map/all_to_all | solution.py:189
  92.9 3.1 %copy-start.7 = (s32[8,16]{1,0:T(8,128)S(1)}, s32[8,16]{1,0:T(8,128)}, u32[]{:S(2)}) copy-start(s32[8,16]{1,0:T(8,128)} %inter_ref.3) | copy-start | bytes 1540
  92.9 3.2 %copy-start.5 = (f32[8,16,16]{2,1,0:T(8,128)S(1)}, f32[8,16,16]{2,1,0:T(8,128)}, u32[]{:S(2)}) copy-start(f32[8,16,16]{2,1,0:T(8,128)} %get-tuple-element.15) | copy-start | bytes 24580
  92.9 3.3 %copy-start.6 = (f32[8,16,16]{2,1,0:T(8,128)S(1)}, f32[8,16,16]{2,1,0:T(8,128)}, u32[]{:S(2)}) copy-start(f32[8,16,16]{2,1,0:T(8,128)} %get-tuple-element.16) | copy-start | bytes 24580
  93.0 33.1 %reduce-scatter.2.cloned.1.call-start = ((), (), s32[]{:S(2)}) async-start(), calls=%async_computation.6 | async-start | bytes 1310720 | tf_op jit(solution)/shard_map/reduce_scatter | solution.py:236
  94.9 1.0 copy-start.2
  96.8 17.2 %collective-permute-start.1 = (f32[1,768]{1,0:T(1,128)S(1)}, f32[1,768]{1,0:T(1,128)S(1)}, u32[]{:S(2)}, u32[]{:S(2)}) collective-permute-start(f32[1,768]{1,0:T(1,128)S(1)} %get-tuple-element.25), channel_id=1, source_target_pairs={{0,2},{1,3},{2,4},{3,5},{4,6},{5,7},{6,0},{7,1},{8,10},{9,11},{10,... | collective-permute-start | bytes 9224 | tf_op jit(solution)/shard_map/ppermute | solution.py:219
  98.6 16.0 %collective-permute-start = (f32[1,768]{1,0:T(1,128)S(1)}, f32[1,768]{1,0:T(1,128)S(1)}, u32[]{:S(2)}, u32[]{:S(2)}) collective-permute-start(f32[1,768]{1,0:T(1,128)S(1)} %get-tuple-element.26), channel_id=1, source_target_pairs={{0,1},{1,2},{2,3},{3,4},{4,5},{5,6},{6,7},{7,0},{8,9},{9,10},{10,1... | collective-permute-start | bytes 9224 | tf_op jit(solution)/shard_map/ppermute | solution.py:219
  98.6 16.8 %collective-permute-start.4 = (f32[1,768]{1,0:T(1,128)S(1)}, f32[1,768]{1,0:T(1,128)S(1)}, u32[]{:S(2)}, u32[]{:S(2)}) collective-permute-start(f32[1,768]{1,0:T(1,128)S(1)} %get-tuple-element.22), channel_id=1, source_target_pairs={{0,5},{1,6},{2,7},{3,0},{4,1},{5,2},{6,3},{7,4},{8,13},{9,14},{10,... | collective-permute-start | bytes 9224 | tf_op jit(solution)/shard_map/ppermute | solution.py:219
  100.1 15.2 %collective-permute-start.2 = (f32[1,768]{1,0:T(1,128)S(1)}, f32[1,768]{1,0:T(1,128)S(1)}, u32[]{:S(2)}, u32[]{:S(2)}) collective-permute-start(f32[1,768]{1,0:T(1,128)S(1)} %get-tuple-element.24), channel_id=1, source_target_pairs={{0,3},{1,4},{2,5},{3,6},{4,7},{5,0},{6,1},{7,2},{8,11},{9,12},{10,... | collective-permute-start | bytes 9224 | tf_op jit(solution)/shard_map/ppermute | solution.py:219
  101.4 14.0 %collective-permute-start.3 = (f32[1,768]{1,0:T(1,128)S(1)}, f32[1,768]{1,0:T(1,128)S(1)}, u32[]{:S(2)}, u32[]{:S(2)}) collective-permute-start(f32[1,768]{1,0:T(1,128)S(1)} %get-tuple-element.23), channel_id=1, source_target_pairs={{0,4},{1,5},{2,6},{3,7},{4,0},{5,1},{6,2},{7,3},{8,12},{9,13},{10,... | collective-permute-start | bytes 9224 | tf_op jit(solution)/shard_map/ppermute | solution.py:219
  114.0 3.6 %collective-permute-start.5 = (f32[1,768]{1,0:T(1,128)S(1)}, f32[1,768]{1,0:T(1,128)S(1)}, u32[]{:S(2)}, u32[]{:S(2)}) collective-permute-start(f32[1,768]{1,0:T(1,128)S(1)} %get-tuple-element.21), channel_id=1, source_target_pairs={{0,6},{1,7},{2,0},{3,1},{4,2},{5,3},{6,4},{7,5},{8,14},{9,15},{10,... | collective-permute-start | bytes 9224 | tf_op jit(solution)/shard_map/ppermute | solution.py:219
  114.6 3.1 %collective-permute-start.6 = (f32[1,768]{1,0:T(1,128)S(1)}, f32[1,768]{1,0:T(1,128)S(1)}, u32[]{:S(2)}, u32[]{:S(2)}) collective-permute-start(f32[1,768]{1,0:T(1,128)S(1)} %get-tuple-element.20), channel_id=1, source_target_pairs={{0,7},{1,0},{2,1},{3,2},{4,3},{5,4},{6,5},{7,6},{8,15},{9,8},{10,9... | collective-permute-start | bytes 9224 | tf_op jit(solution)/shard_map/ppermute | solution.py:219
  121.3 20.3 %all-to-all-start.4 = ((bf16[4,272,256]{2,1,0:T(8,128)(2,1)}), bf16[4,272,256]{2,1,0:T(8,128)(2,1)S(1)}, u32[]{:S(2)}, u32[]{:S(2)}) async-start(bf16[4,272,256]{2,1,0:T(8,128)(2,1)} %sum_galaxies.2), calls=%async_computation.4 | async-start | bytes 1114112 | tf_op jit(solution)/shard_map/all_to_all | solution.py:240
Sparse Core Ops, SparseCore 0:
  96.1 28.7 reduce-scatter.1
